TPU v7x, 512 devices: a whole 4x8x8 slice. The times are simulated.
512 devices in a mesh: train: 128 (over z, y, core), feat: 4 (over x).
Axes of the slice: x: 4, y: 8, z: 8, core: 2. Of those that a mesh axis runs over, the one named last changes fastest.
Arguments:
- train_feats: bfloat16 [262144, 2048], P('train', 'feat'), may hold values from -180 to 180, as said below
- test_feats: bfloat16 [512, 2048], P('feat'), may hold values from -180 to 180, as said below
Outputs:
- scores: bfloat16 [262144, 512], P('train', 'feat')
Inputs may be any that keep to these rules, and one draw needn't show every extreme that they name: `train_feats`: each training example has its own scale. `test_feats`: each test example has its own scale.
All inputs are finite; a program needn't handle non-finite values.
Results may differ from a plain program's by a relative error of at most 0.0058.
Values may be sent and summed in bfloat16 or wider, within the bound.
No kernel may reach another device: no remote copies, remote signals or barrier semaphores. Data moves between devices by JAX's collectives and lax.ppermute only.
A program may use at most 64 MiB of HBM per device.

v0:
```python
import jax
import jax.numpy as jnp
from jax import lax
from jax.sharding import PartitionSpec as P

ITERS = 2


damping = 0.05


def local(train_feats, test_feats):
    whole = lax.all_gather(train_feats, "feat", axis=1, tiled=True)
    width = whole.shape[1]
    total_rows = whole.shape[0] * lax.axis_size("train")
    energy = lax.psum(jnp.sum(jnp.square(whole.astype(jnp.float32)), axis=0), "train")
    diag_full = energy[:, None] / total_rows + damping
    rhs_full = test_feats.astype(jnp.float32).T

    def norm_sum(values):
        return jnp.sum(values, axis=0)

    solution = jnp.zeros_like(rhs_full)
    resid = rhs_full
    precond = resid / diag_full
    search = precond
    rz_now = norm_sum(resid * precond)
    for step in range(ITERS):
        prod = jnp.dot(whole, search.astype(jnp.bfloat16), preferred_element_type=jnp.float32)
        back = jnp.einsum(
            "np,nm->pm", whole, prod.astype(jnp.bfloat16), preferred_element_type=jnp.float32
        )
        image = lax.psum(back, "train") / total_rows + damping * search
        alpha = rz_now / jnp.sum(search * image, axis=0)
        solution = solution + alpha * search
        resid = resid - alpha * image
        precond = resid / diag_full
        rz_next = norm_sum(resid * precond)
        search = precond + rz_next / rz_now * search
        rz_now = rz_next
    solution_b = solution.astype(jnp.bfloat16)
    out = jnp.dot(whole, solution_b, preferred_element_type=jnp.float32)
    return (out * (1.0 / jnp.sqrt(jnp.float32(width)))).astype(jnp.bfloat16)


def solution(mesh):
    return jax.shard_map(
        local,
        mesh=mesh,
        in_specs=(P("train", "feat"), P("feat", None)),
        out_specs=P("train", "feat"),
        check_vma=False,
    )
```

profile of v0, /device:TPU:1, one launch (start us, length us, event | category | flops | bytes accessed | tf_op | source)
XLA Modules:
  0.0 787.6 jit_solution(2693315294164273648)
XLA Ops:
  6.5 0.0 copy-start.1
  6.5 0.0 all-gather.2.cloned.1.call-start
  6.5 0.7 all-gather.2.cloned.1.call-update
  7.3 0.0 all-reduce.3.cloned.1.call-start
  7.3 96.1 %all-gather.2.cloned.1.call-done = bf16[2048,2048]{1,0:T(8,128)(2,1)} async-done(((bf16[2048,512]{1,0:T(8,128)(2,1)}), bf16[2048,2048]{1,0:T(8,128)(2,1)}) %all-gather.2.cloned.1.call-update) | async-done | bytes 8388624 | tf_op jit(solution)/shard_map/all_gather | solution.py:13
  103.4 5.1 multiply_reduce_fusion
  108.5 252.2 %psum.21 = f32[2048]{0:T(1024)S(1)} all-reduce(f32[2048]{0:T(1024)S(1)} %multiply_reduce_fusion), channel_id=1, replica_groups=mesh['train'=128,'feat'=4] {'train'}, use_global_device_ids=true, to_apply=%region_1.0 | all-reduce | flops 2048 | bytes 16384 | tf_op jit(solution)/shard_map/psum | solution.py:16
  360.7 0.0 copy-done.1
  360.7 10.7 %convolution_bitcast_fusion.1 = f32[2048,128]{0,1:T(8,128)} fusion(bf16[2048,2048]{1,0:T(8,128)(2,1)} %all-gather.2.cloned.1.call-done, bf16[128,2048]{1,0:T(8,128)(2,1)S(1)} %copy-done.1, f32[2048]{0:T(1024)S(1)} %multiply_add_fusion.2), kind=kOutput, calls=%fused_computation.2 | convolution fusion | flops 2148532224 | bytes 9969664 | tf_op jit(solution)/shard_map/np,nm->pm/dot_general | solution.py:30
  371.5 0.0 all-reduce.3.cloned.1.call-update
  371.5 0.2 all-reduce.5.cloned.1.call-start
  371.7 192.3 %all-reduce.3.cloned.1.call-done = f32[2048,128]{0,1:T(8,128)} async-done(((f32[2048,128]{0,1:T(8,128)}), f32[2048,128]{0,1:T(8,128)}) %all-reduce.3.cloned.1.call-update) | async-done | bytes 1048592 | tf_op jit(solution)/shard_map/psum | solution.py:33
  564.0 1.6 multiply_reduce_fusion.3
  565.7 1.7 multiply_reduce_fusion.2
  567.4 0.0 copy-start
  567.4 11.2 %convolution_bitcast_fusion = f32[2048,128]{0,1:T(8,128)} fusion(bf16[2048,2048]{1,0:T(8,128)(2,1)} %all-gather.2.cloned.1.call-done, f32[128]{0:T(128)S(1)} %div.54, f32[2048]{0:T(1024)S(1)} %multiply_add_fusion.2, f32[2048,128]{0,1:T(8,128)} %all-reduce.3.cloned.1.call-done, f32[128]{0:T(128)S(1)} %div.52, bf16[128,2048]{1,0:T(8,128)(2,1)S(1)} %copy-done.1), kind=kOutput, calls=%fused_computation.1 | convolution fusion | flops 2150629376 | bytes 11019264 | tf_op jit(solution)/shard_map/np,nm->pm/dot_general | solution.py:30
  578.6 0.0 all-reduce.5.cloned.1.call-update
  578.6 193.2 %all-reduce.5.cloned.1.call-done = f32[2048,128]{0,1:T(8,128)} async-done(((f32[2048,128]{0,1:T(8,128)}), f32[2048,128]{0,1:T(8,128)}) %all-reduce.5.cloned.1.call-update) | async-done | bytes 1048592 | tf_op jit(solution)/shard_map/psum | solution.py:33
  771.8 0.0 copy-done
  771.8 1.9 multiply_reduce_fusion.1
  773.7 6.4 fusion.1
  780.1 1.0 copy.3
  (4 shorter events, 0.0 us)
Async XLA Ops:
  6.5 354.2 %copy-start.1 = (bf16[128,2048]{1,0:T(8,128)(2,1)S(1)}, bf16[128,2048]{1,0:T(8,128)(2,1)}, u32[]{:S(2)}) copy-start(bf16[128,2048]{1,0:T(8,128)(2,1)} %param.3) | copy-start | bytes 1572868
  6.5 96.9 %all-gather.2.cloned.1.call-start = ((), (), s32[]{:S(2)}) async-start(), calls=%async_computation | async-start | bytes 10485760 | tf_op jit(solution)/shard_map/all_gather | solution.py:13
  7.3 556.8 %all-reduce.3.cloned.1.call-start = ((), (), s32[]{:S(2)}) async-start(), calls=%async_computation.1 | async-start | bytes 2097152 | tf_op jit(solution)/shard_map/psum | solution.py:33
  371.5 400.3 %all-reduce.5.cloned.1.call-start = ((), (), s32[]{:S(2)}) async-start(), calls=%async_computation.2 | async-start | bytes 2097152 | tf_op jit(solution)/shard_map/psum | solution.py:33
  567.4 204.4 %copy-start = (f32[2048,128]{0,1:T(8,128)S(1)}, f32[2048,128]{0,1:T(8,128)}, u32[]{:S(2)}) copy-start(f32[2048,128]{0,1:T(8,128)} %all-reduce.3.cloned.1.call-done) | copy-start | bytes 3145732
Sparse Core Ops, SparseCore 0:
  9.5 93.8 all-gather.1
  371.6 192.3 all-reduce.2
  578.7 193.0 all-reduce.4
where the time goes:
time: 789 us; the launch traced here: 788 us
  waiting for transfers between devices  482 us (61%)
  blocking collectives  252 us (32%)
  matrix products  28.3 us (4%)
  between operations  13.2 us (2%)
  other arithmetic  10.3 us (1%)
    psum x2, waiting for transfers between devices, local(): image = lax.psum(back, 'train') / total_rows + damping * search  385 us
    psum x1, blocking collectives, local(): lax.psum(jnp.sum(jnp.square(whole.astype(jnp.float32)), axis=0), 'train')  252 us
    all_gather x1, waiting for transfers between devices, local(): whole = lax.all_gather(train_feats, 'feat', axis=1, tiled=True)  96.1 us
    dot_general x2, matrix products, local(): jnp.einsum('np,nm->pm', whole, prod.astype(jnp.bfloat16), preferred_eleme...  21.9 us
  transfers between devices with their start and end apart: 3, of which 3 were waited for; matrix products, arithmetic and copies ran while one was open for 0% of the time, Pallas kernels for 0%

commit v1 on v0

v1 whole, which is shorter than its diff:
```python
import jax
import jax.numpy as jnp
from jax import lax
from jax.sharding import PartitionSpec as P

damping = 0.05
bf16 = jnp.bfloat16
f32 = jnp.float32


def ring(size, step):
    return [(i, (i + step) % size) for i in range(size)]


def everyone(value, axis, count):
    return lax.all_to_all(jnp.broadcast_to(value[None], (count,) + value.shape), axis, 0, 0, tiled=True)


def split3(value):
    first = lax.reduce_precision(value, 8, 7)
    second = lax.reduce_precision(value - first, 8, 7)
    third = value - first - second
    return first.astype(bf16), second.astype(bf16), third.astype(bf16)


def local(train_feats, test_feats):
    rows, block = train_feats.shape
    tests, width = test_feats.shape
    feats = lax.axis_size("feat")
    members = lax.axis_size("train")
    total_rows = rows * members
    half = rows // 2
    me = lax.axis_index("feat")
    owner = lax.axis_index("train")
    right, left = ring(feats, 1), ring(feats, -1)

    low, high = train_feats[:half], train_feats[half:]
    prev_low = lax.ppermute(low, "feat", right)
    next_high = lax.ppermute(high, "feat", left)
    prev_high = lax.ppermute(high, "feat", right)
    next_low = lax.ppermute(low, "feat", left)
    far_low = lax.ppermute(prev_low, "feat", right)
    far_high = lax.ppermute(next_high, "feat", left)

    order = [me, (me + feats - 1) % feats, (me + 1) % feats, (me + 2) % feats]
    energy = jnp.sum(jnp.square(train_feats.astype(f32)), axis=0).reshape(block // 128, 128)
    energy = jnp.sum(everyone(energy, "train", members), axis=0)
    energy = everyone(energy, "feat", feats)
    diag = jnp.concatenate([lax.dynamic_index_in_dim(energy, o, 0, False) for o in order], 0)
    diag = diag / total_rows + damping
    rhs = jnp.concatenate([lax.dynamic_slice_in_dim(test_feats, o * block, block, 1) for o in order], 1)
    rhs = rhs.astype(f32)
    search0 = rhs / diag.reshape(1, width)
    dir0 = search0.astype(bf16).T

    halves = [
        (low, prev_low, next_low, far_low),
        (high, prev_high, next_high, far_high),
    ]

    def forward(direction):
        out = []
        for parts in halves:
            total = 0.0
            for i, part in enumerate(parts):
                total = total + jnp.dot(part, direction[i * block:(i + 1) * block], preferred_element_type=f32)
            out.append(total)
        return out

    prod = [p.astype(bf16) for p in forward(dir0)]
    back = [
        sum(
            jnp.einsum("nm,np->mp", prod[h], halves[h][i], preferred_element_type=f32)
            for h in range(2)
        )
        for i in range(4)
    ]
    back = jnp.concatenate(back, 1).astype(bf16).reshape(tests, width // 128, 128)
    back = lax.all_to_all(back, "train", 0, 0, tiled=True)
    back = jnp.sum(back.astype(f32), axis=0)

    mine = lax.dynamic_index_in_dim(rhs, owner, 0, False).reshape(width // 128, 128)
    precond = mine / diag
    rz0 = jnp.sum(mine * precond)
    image = back / total_rows + damping * precond
    alpha0 = rz0 / jnp.sum(precond * image)
    resid = mine - alpha0 * image
    precond1 = resid / diag
    rz1 = jnp.sum(resid * precond1)
    search1 = precond1 + rz1 / rz0 * precond
    norm1 = jnp.sum(search1 * search1)
    scalars = jnp.stack([jnp.stack(split3(s)) for s in (alpha0, rz1, norm1)]).reshape(9)
    extra = jnp.zeros((8, 128), bf16).at[0, :9].set(scalars)
    message = jnp.concatenate([search1.astype(bf16), extra], 0)
    message = everyone(message, "train", members)
    dir1t = message[:, : width // 128].reshape(tests, width)
    dir1 = dir1t.T
    pieces = message[:, width // 128, :9].astype(f32).reshape(tests, 3, 3)
    alpha0, rz1, norm1 = jnp.sum(pieces, axis=2).T

    prod1 = forward(dir1)
    square = sum(jnp.sum(p * p, axis=0) for p in prod1)
    square = jnp.sum(everyone(square.reshape(1, tests), "train", members), axis=(0, 1))
    alpha1 = rz1 / (square / total_rows + damping * norm1)
    answer = alpha0[:, None] * search0 + alpha1[:, None] * dir1t.astype(f32)
    out = forward(answer.astype(bf16).T)
    scale = 1.0 / jnp.sqrt(f32(width))
    return jnp.concatenate([(o * scale).astype(bf16) for o in out], 0)


def solution(mesh):
    return jax.shard_map(
        local,
        mesh=mesh,
        in_specs=(P("train", "feat"), P("feat", None)),
        out_specs=P("train", "feat"),
        check_vma=False,
    )
```

time: 789 us -> 270 us (0.34)
  waiting for transfers between devices: 482 us -> 78.4 us
  blocking collectives: 252 us -> 31.1 us
  starting transfers between devices: 0.26 us -> 66.1 us
  local copies, waits for them, and re-layouts: 1.01 us -> 19.9 us
  other arithmetic: 10.3 us -> 20.7 us
  matrix products: 28.3 us -> 36.2 us
    psum x2 -> x0, waiting for transfers between devices: 385 us -> none  [local(): image = lax.psum(back, 'train') / total_rows + damping * search]
    psum x1 -> x0, blocking collectives: 252 us -> none  [local(): lax.psum(jnp.sum(jnp.square(whole.astype(jnp.float32)), axis=0), 'train')]
    all_gather x1 -> x0, waiting for transfers between devices: 96.1 us -> none  [local(): whole = lax.all_gather(train_feats, 'feat', axis=1, tiled=True)]
    all_to_all x0 -> x4, waiting for transfers between devices: none -> 60.4 us  [the longest x3 42.2 us: everyone(): lax.all_to_all(jnp.broadcast_to(value[None], (count,) + value.shape), axi...]
    all_to_all x0 -> x4, starting transfers between devices: none -> 46.5 us  [the longest x3 28.8 us: everyone(): lax.all_to_all(jnp.broadcast_to(value[None], (count,) + value.shape), axi...]
    all_to_all x0 -> x1, blocking collectives: none -> 31.1 us  [everyone(): lax.all_to_all(jnp.broadcast_to(value[None], (count,) + value.shape), axi...]
    ppermute x0 -> x6, starting transfers between devices: none -> 19.5 us  [the longest x1 4.61 us: local(): far_high = lax.ppermute(next_high, 'feat', left)]
    ppermute x0 -> x6, waiting for transfers between devices: none -> 18.1 us  [the longest x1 18 us: local(): far_low = lax.ppermute(prev_low, 'feat', right)]
  transfers between devices with their start and end apart: 3 -> 10, of which waited for: 3 -> 5; matrix products, arithmetic and copies ran while one was open for 0% -> 6% of each run, Pallas kernels for 0% -> 0%
where the time goes in v1:
time: 270 us; the launch traced here: 269 us
  waiting for transfers between devices  78.4 us (29%)
  starting transfers between devices  66.1 us (24%)
  matrix products  36.2 us (13%)
  blocking collectives  31.1 us (12%)
  other arithmetic  20.7 us (8%)
  local copies, waits for them, and re-layouts  19.9 us (7%)
  between operations  16.3 us (6%)
    all_to_all x3, waiting for transfers between devices, everyone(): lax.all_to_all(jnp.broadcast_to(value[None], (count,) + value.shape), axi...  42.2 us
    all_to_all x1, blocking collectives, everyone(): lax.all_to_all(jnp.broadcast_to(value[None], (count,) + value.shape), axi...  31.1 us
    all_to_all x3, starting transfers between devices, everyone(): lax.all_to_all(jnp.broadcast_to(value[None], (count,) + value.shape), axi...  28.8 us
    dot_general x24, matrix products, forward(): jnp.dot(part, direction[i * block:(i + 1) * block], preferred_element_typ...  24.6 us
    all_to_all x1, waiting for transfers between devices, local(): back = lax.all_to_all(back, 'train', 0, 0, tiled=True)  18.2 us
    ppermute x1, waiting for transfers between devices, local(): far_low = lax.ppermute(prev_low, 'feat', right)  18 us
    all_to_all x1, starting transfers between devices, local(): back = lax.all_to_all(back, 'train', 0, 0, tiled=True)  17.7 us
    dot_general x8, matrix products, local(): jnp.einsum('nm,np->mp', prod[h], halves[h][i], preferred_element_type=f32)  11.6 us
  transfers between devices with their start and end apart: 10, of which 5 were waited for; matrix products, arithmetic and copies ran while one was open for 6% of the time, Pallas kernels for 0%

profile of v1, /device:TPU:1, one launch (start us, length us, event | category | flops | bytes accessed | tf_op | source)
XLA Modules:
  0.0 268.7 jit_solution(8292580745000051359)
XLA Ops:
  0.0 2.2 multiply_reduce_fusion
  3.0 18.4 %all-to-all-start = ((f32[128,4,128]{2,1,0:T(4,128)}), f32[128,4,128]{2,1,0:T(4,128)S(1)}, u32[]{:S(2)}, u32[]{:S(2)}) async-start(f32[128,4,128]{2,1,0:T(4,128)} %broadcast_in_dim.11), calls=%async_computation | async-start | bytes 524288 | tf_op jit(solution)/shard_map/all_to_all | solution.py:16
  22.9 3.1 %collective-permute-start.3 = (bf16[1024,512]{1,0:T(8,128)(2,1)}, bf16[1024,512]{1,0:T(8,128)(2,1)S(1)}, u32[]{:S(2)}, u32[]{:S(2)}) collective-permute-start(bf16[1024,512]{1,0:T(8,128)(2,1)} %get-tuple-element.24), channel_id=1, source_target_pairs={{0,1},{1,2},{2,3},{3,0},{4,5},{5,6},{6,7},{7,4},{8,9},{9,10},{10,1... | collective-permute-start | bytes 3145736 | tf_op jit(solution)/shard_map/ppermute | solution.py:40
  26.0 3.4 %collective-permute-start.4 = (bf16[1024,512]{1,0:T(8,128)(2,1)}, bf16[1024,512]{1,0:T(8,128)(2,1)}, u32[]{:S(2)}, u32[]{:S(2)}) collective-permute-start(bf16[1024,512]{1,0:T(8,128)(2,1)} %get-tuple-element.24), channel_id=1, source_target_pairs={{0,3},{1,0},{2,1},{3,2},{4,7},{5,4},{6,5},{7,6},{8,11},{9,8},{10,9... | collective-permute-start | bytes 3145736 | tf_op jit(solution)/shard_map/ppermute | solution.py:39
  29.4 1.9 collective-permute-start
  31.3 4.6 %collective-permute-start.1 = (bf16[1024,512]{1,0:T(8,128)(2,1)}, bf16[1024,512]{1,0:T(8,128)(2,1)}, u32[]{:S(2)}, u32[]{:S(2)}) collective-permute-start(bf16[1024,512]{1,0:T(8,128)(2,1)} %get-tuple-element.23), channel_id=1, source_target_pairs={{0,3},{1,0},{2,1},{3,2},{4,7},{5,4},{6,5},{7,6},{8,11},{9,8},{10,9... | collective-permute-start | bytes 3145736 | tf_op jit(solution)/shard_map/ppermute | solution.py:41
  37.4 4.0 %all-to-all-start.1 = ((f32[4,4,128]{2,1,0:T(4,128)}), f32[4,4,128]{2,1,0:T(4,128)S(1)}, u32[]{:S(2)}, u32[]{:S(2)}) async-start(f32[4,4,128]{2,1,0:T(4,128)} %broadcast_in_dim.12), calls=%async_computation.1 | async-start | bytes 16384 | tf_op jit(solution)/shard_map/all_to_all | solution.py:16
  43.2 31.0 %all-to-all-done.1 = f32[4,4,128]{2,1,0:T(4,128)S(1)} async-done(((f32[4,4,128]{2,1,0:T(4,128)}), f32[4,4,128]{2,1,0:T(4,128)S(1)}, u32[]{:S(2)}, u32[]{:S(2)}) %all-to-all-start.1) | async-done | bytes 8224 | tf_op jit(solution)/shard_map/all_to_all | solution.py:16
  76.9 4.6 %collective-permute-start.5 = (bf16[1024,512]{1,0:T(8,128)(2,1)}, bf16[1024,512]{1,0:T(8,128)(2,1)S(1)}, u32[]{:S(2)}, u32[]{:S(2)}) collective-permute-start(bf16[1024,512]{1,0:T(8,128)(2,1)} %collective-permute-done.4), channel_id=1, source_target_pairs={{0,3},{1,0},{2,1},{3,2},{4,7},{5,4},{6,5},{7,6},{8,11},{9,8},{10,9... | collective-permute-start | bytes 3145736 | tf_op jit(solution)/shard_map/ppermute | solution.py:43
  81.5 1.9 collective-permute-start.2
  89.1 18.0 %collective-permute-done.2 = bf16[1024,512]{1,0:T(8,128)(2,1)S(1)} collective-permute-done((bf16[1024,512]{1,0:T(8,128)(2,1)}, bf16[1024,512]{1,0:T(8,128)(2,1)S(1)}, u32[]{:S(2)}, u32[]{:S(2)}) %collective-permute-start.2) | collective-permute-done | bytes 1048608 | tf_op jit(solution)/shard_map/ppermute | solution.py:42
  114.5 2.2 fusion.14
  119.5 2.2 fusion.13
  123.3 2.0 fusion.12
  127.0 2.3 pad_maximum_fusion
  129.2 17.7 %all-to-all-start.2 = ((bf16[128,16,128]{2,1,0:T(8,128)(2,1)}), bf16[128,16,128]{2,1,0:T(8,128)(2,1)}, u32[]{:S(2)}, u32[]{:S(2)}) async-start(bf16[128,16,128]{2,1,0:T(8,128)(2,1)} %pad_maximum_fusion), calls=%async_computation.2 | async-start | bytes 1048576 | tf_op jit(solution)/shard_map/all_to_all | solution.py:79
  147.0 2.0 maximum_convert_fusion
  149.0 18.2 %all-to-all-done.2 = bf16[128,16,128]{2,1,0:T(8,128)(2,1)} async-done(((bf16[128,16,128]{2,1,0:T(8,128)(2,1)}), bf16[128,16,128]{2,1,0:T(8,128)(2,1)}, u32[]{:S(2)}, u32[]{:S(2)}) %all-to-all-start.2) | async-done | bytes 524320 | tf_op jit(solution)/shard_map/all_to_all | solution.py:79
  169.0 2.1 multiply_reduce_fusion.3
  172.4 2.0 multiply_reduce_fusion.2
  193.6 31.1 %all_to_all.25 = bf16[128,24,128]{2,1,0:T(8,128)(2,1)S(1)} all-to-all(bf16[128,24,128]{2,1,0:T(8,128)(2,1)S(1)} %broadcast_in_dim.13), channel_id=1, replica_groups=mesh['train'=128,'feat'=4] {'train'}, dimensions={0} | all-to-all | bytes 1572864 | tf_op jit(solution)/shard_map/all_to_all | solution.py:16
  232.5 2.0 convolution_add_fusion.11
  240.4 6.4 %all-to-all-start.4 = ((f32[128,1,128]{2,1,0:T(1,128)}), f32[128,1,128]{2,1,0:T(1,128)}, u32[]{:S(2)}, u32[]{:S(2)}) async-start(f32[128,1,128]{2,1,0:T(1,128)} %broadcast_in_dim.14), calls=%async_computation.4 | async-start | bytes 131072 | tf_op jit(solution)/shard_map/all_to_all | solution.py:16
  247.3 10.4 %all-to-all-done.4 = f32[128,1,128]{2,1,0:T(1,128)} async-done(((f32[128,1,128]{2,1,0:T(1,128)}), f32[128,1,128]{2,1,0:T(1,128)}, u32[]{:S(2)}, u32[]{:S(2)}) %all-to-all-start.4) | async-done | bytes 65568 | tf_op jit(solution)/shard_map/all_to_all | solution.py:16
  (113 shorter events, 58.6 us)
Async XLA Ops:
  0.0 21.4 %copy-start = (bf16[2048,512]{1,0:T(8,128)(2,1)S(1)}, bf16[2048,512]{1,0:T(8,128)(2,1)}, u32[]{:S(2)}) copy-start(bf16[2048,512]{1,0:T(8,128)(2,1)} %param.4) | copy-start | bytes 6291460
  3.0 33.7 %all-to-all-start = ((f32[128,4,128]{2,1,0:T(4,128)}), f32[128,4,128]{2,1,0:T(4,128)S(1)}, u32[]{:S(2)}, u32[]{:S(2)}) async-start(f32[128,4,128]{2,1,0:T(4,128)} %broadcast_in_dim.11), calls=%async_computation | async-start | bytes 524288 | tf_op jit(solution)/shard_map/all_to_all | solution.py:16
  22.9 60.5 %collective-permute-start.3 = (bf16[1024,512]{1,0:T(8,128)(2,1)}, bf16[1024,512]{1,0:T(8,128)(2,1)S(1)}, u32[]{:S(2)}, u32[]{:S(2)}) collective-permute-start(bf16[1024,512]{1,0:T(8,128)(2,1)} %get-tuple-element.24), channel_id=1, source_target_pairs={{0,1},{1,2},{2,3},{3,0},{4,5},{5,6},{6,7},{7,4},{8,9},{9,10},{10,1... | collective-permute-start | bytes 3145736 | tf_op jit(solution)/shard_map/ppermute | solution.py:40
  26.0 50.9 %collective-permute-start.4 = (bf16[1024,512]{1,0:T(8,128)(2,1)}, bf16[1024,512]{1,0:T(8,128)(2,1)}, u32[]{:S(2)}, u32[]{:S(2)}) collective-permute-start(bf16[1024,512]{1,0:T(8,128)(2,1)} %get-tuple-element.24), channel_id=1, source_target_pairs={{0,3},{1,0},{2,1},{3,2},{4,7},{5,4},{6,5},{7,6},{8,11},{9,8},{10,9... | collective-permute-start | bytes 3145736 | tf_op jit(solution)/shard_map/ppermute | solution.py:39
  29.4 52.1 %collective-permute-start = (bf16[1024,512]{1,0:T(8,128)(2,1)}, bf16[1024,512]{1,0:T(8,128)(2,1)}, u32[]{:S(2)}, u32[]{:S(2)}) collective-permute-start(bf16[1024,512]{1,0:T(8,128)(2,1)} %get-tuple-element.23), channel_id=1, source_target_pairs={{0,1},{1,2},{2,3},{3,0},{4,5},{5,6},{6,7},{7,4},{8,9},{9,10},{10,1... | collective-permute-start | bytes 3145736 | tf_op jit(solution)/shard_map/ppermute | solution.py:38
  31.3 56.0 %collective-permute-start.1 = (bf16[1024,512]{1,0:T(8,128)(2,1)}, bf16[1024,512]{1,0:T(8,128)(2,1)}, u32[]{:S(2)}, u32[]{:S(2)}) collective-permute-start(bf16[1024,512]{1,0:T(8,128)(2,1)} %get-tuple-element.23), channel_id=1, source_target_pairs={{0,3},{1,0},{2,1},{3,2},{4,7},{5,4},{6,5},{7,6},{8,11},{9,8},{10,9... | collective-permute-start | bytes 3145736 | tf_op jit(solution)/shard_map/ppermute | solution.py:41
  37.4 36.8 %all-to-all-start.1 = ((f32[4,4,128]{2,1,0:T(4,128)}), f32[4,4,128]{2,1,0:T(4,128)S(1)}, u32[]{:S(2)}, u32[]{:S(2)}) async-start(f32[4,4,128]{2,1,0:T(4,128)} %broadcast_in_dim.12), calls=%async_computation.1 | async-start | bytes 16384 | tf_op jit(solution)/shard_map/all_to_all | solution.py:16
  43.2 33.6 %copy-start.12 = (bf16[128,512]{1,0:T(8,128)(2,1)}, bf16[128,512]{1,0:T(8,128)(2,1)S(1)}, u32[]{:S(2)}) copy-start(bf16[128,512]{1,0:T(8,128)(2,1)S(1)} %get-tuple-element.26) | copy-start | bytes 393220
  43.2 33.6 %copy-start.14 = (bf16[128,512]{1,0:T(8,128)(2,1)}, bf16[128,512]{1,0:T(8,128)(2,1)S(1)}, u32[]{:S(2)}) copy-start(bf16[128,512]{1,0:T(8,128)(2,1)S(1)} %get-tuple-element.27) | copy-start | bytes 393220
  76.9 31.7 %collective-permute-start.5 = (bf16[1024,512]{1,0:T(8,128)(2,1)}, bf16[1024,512]{1,0:T(8,128)(2,1)S(1)}, u32[]{:S(2)}, u32[]{:S(2)}) collective-permute-start(bf16[1024,512]{1,0:T(8,128)(2,1)} %collective-permute-done.4), channel_id=1, source_target_pairs={{0,3},{1,0},{2,1},{3,2},{4,7},{5,4},{6,5},{7,6},{8,11},{9,8},{10,9... | collective-permute-start | bytes 3145736 | tf_op jit(solution)/shard_map/ppermute | solution.py:43
  81.5 25.6 %collective-permute-start.2 = (bf16[1024,512]{1,0:T(8,128)(2,1)}, bf16[1024,512]{1,0:T(8,128)(2,1)S(1)}, u32[]{:S(2)}, u32[]{:S(2)}) collective-permute-start(bf16[1024,512]{1,0:T(8,128)(2,1)} %collective-permute-done), channel_id=1, source_target_pairs={{0,1},{1,2},{2,3},{3,0},{4,5},{5,6},{6,7},{7,4},{8,9},{9,10},{10,1... | collective-permute-start | bytes 3145736 | tf_op jit(solution)/shard_map/ppermute | solution.py:42
  107.1 2.8 %copy-start.4 = (bf16[1024,512]{1,0:T(8,128)(2,1)}, bf16[1024,512]{1,0:T(8,128)(2,1)S(1)}, u32[]{:S(2)}) copy-start(bf16[1024,512]{1,0:T(8,128)(2,1)S(1)} %collective-permute-done.2) | copy-start | bytes 3145732
  108.6 1.0 copy-start.1
  123.3 23.6 %copy-start.13 = (bf16[128,512]{1,0:T(8,128)(2,1)S(1)}, bf16[128,512]{1,0:T(8,128)(2,1)}, u32[]{:S(2)}) copy-start(bf16[128,512]{1,0:T(8,128)(2,1)} %copy-done.12) | copy-start | bytes 393220
  123.3 23.6 %copy-start.15 = (bf16[128,512]{1,0:T(8,128)(2,1)S(1)}, bf16[128,512]{1,0:T(8,128)(2,1)}, u32[]{:S(2)}) copy-start(bf16[128,512]{1,0:T(8,128)(2,1)} %copy-done.14) | copy-start | bytes 393220
  129.2 37.9 %all-to-all-start.2 = ((bf16[128,16,128]{2,1,0:T(8,128)(2,1)}), bf16[128,16,128]{2,1,0:T(8,128)(2,1)}, u32[]{:S(2)}, u32[]{:S(2)}) async-start(bf16[128,16,128]{2,1,0:T(8,128)(2,1)} %pad_maximum_fusion), calls=%async_computation.2 | async-start | bytes 1048576 | tf_op jit(solution)/shard_map/all_to_all | solution.py:79
  225.7 1.3 copy-start.7
  232.5 2.0 copy-start.8
  232.5 3.8 %copy-start.5 = (bf16[1024,512]{1,0:T(8,128)(2,1)S(1)}, bf16[1024,512]{1,0:T(8,128)(2,1)}, u32[]{:S(2)}) copy-start(bf16[1024,512]{1,0:T(8,128)(2,1)} %copy-done.4) | copy-start | bytes 3145732
  234.6 2.3 copy-start.11
  236.9 2.2 copy-start.2
  240.4 17.4 %all-to-all-start.4 = ((f32[128,1,128]{2,1,0:T(1,128)}), f32[128,1,128]{2,1,0:T(1,128)}, u32[]{:S(2)}, u32[]{:S(2)}) async-start(f32[128,1,128]{2,1,0:T(1,128)} %broadcast_in_dim.14), calls=%async_computation.4 | async-start | bytes 131072 | tf_op jit(solution)/shard_map/all_to_all | solution.py:16
  260.9 2.2 copy-start.3
  263.6 3.5 %copy-start.6 = (bf16[1024,512]{1,0:T(8,128)(2,1)S(1)}, bf16[1024,512]{1,0:T(8,128)(2,1)}, u32[]{:S(2)}) copy-start(bf16[1024,512]{1,0:T(8,128)(2,1)} %copy-done.4) | copy-start | bytes 3145732
  (7 other events, 4.7 us)

commit v2 on v0

v2 whole, which is shorter than its diff:
```python
import functools

import jax
import jax.numpy as jnp
from jax import lax
from jax.experimental import pallas as pl
from jax.experimental.pallas import tpu as pltpu
from jax.sharding import PartitionSpec as P

damping = 0.05
bf16 = jnp.bfloat16
f32 = jnp.float32
LANES = 128
TILE = 256
VMEM_BYTES = 20 * 1024 * 1024


def ring(size, step):
    return [(i, (i + step) % size) for i in range(size)]


def everyone(value, axis, count):
    return lax.all_to_all(jnp.broadcast_to(value[None], (count,) + value.shape), axis, 0, 0, tiled=True)


def times(parts, direction_ref):
    total = None
    for i, part in enumerate(parts):
        block = part.shape[1]
        term = jnp.dot(part[...], direction_ref[i * block:(i + 1) * block, :], preferred_element_type=f32)
        total = term if total is None else total + term
    return total


def first_kernel(*refs):
    low, high = refs[0:4], refs[4:8]
    direction, back, prod_low, prod_high, norm, total, spread = refs[8:]
    step = pl.program_id(0)

    @pl.when(step == 0)
    def _():
        total[...] = jnp.zeros_like(total)
        norm[...] = jnp.zeros_like(norm)

    block = low[0].shape[1]
    for parts, prod in ((low, prod_low), (high, prod_high)):
        value = times(parts, direction)
        prod[...] = value
        norm[...] += jnp.sum(value * value, axis=0, keepdims=True)
        turned = value.T.astype(bf16)
        for i, part in enumerate(parts):
            total[:, i * block:(i + 1) * block] += jnp.dot(turned, part[...], preferred_element_type=f32)

    @pl.when(step == pl.num_programs(0) - 1)
    def _():
        count = total.shape[1] // LANES
        tests = total.shape[0]
        for j in range(count):
            spread[pl.ds(j, tests, stride=count), :] = total[:, j * LANES:(j + 1) * LANES]
        back[...] = spread[...].astype(bf16)


def first(low, high, direction):
    rows, block = low[0].shape
    width, tests = direction.shape
    tile = pl.BlockSpec((TILE, block), lambda i: (i, 0))
    out = pl.BlockSpec((TILE, tests), lambda i: (i, 0))
    whole = lambda *shape: pl.BlockSpec(shape, lambda i: (0, 0))
    count = width // LANES
    return pl.pallas_call(
        first_kernel,
        grid=(rows // TILE,),
        in_specs=[tile] * 8 + [whole(width, tests)],
        out_specs=[whole(tests * count, LANES), out, out, whole(1, tests)],
        out_shape=[
            jax.ShapeDtypeStruct((tests * count, LANES), bf16),
            jax.ShapeDtypeStruct((rows, tests), f32),
            jax.ShapeDtypeStruct((rows, tests), f32),
            jax.ShapeDtypeStruct((1, tests), f32),
        ],
        scratch_shapes=[pltpu.VMEM((tests, width), f32), pltpu.VMEM((tests * count, LANES), f32)],
        compiler_params=pltpu.CompilerParams(vmem_limit_bytes=VMEM_BYTES),
        cost_estimate=pl.CostEstimate(flops=8 * rows * width * tests, bytes_accessed=4 * rows * width, transcendentals=0),
        name="first",
    )(*low, *high, direction)


def column_kernel(total_rows, parts, diag_ref, mine_ref, out):
    diag, mine = diag_ref[...], mine_ref[...]

    def dot(a, b):
        return jnp.sum(jnp.sum(a * b, axis=0, keepdims=True), axis=1, keepdims=True)

    back = jnp.sum(parts[...].astype(f32), axis=0)
    precond = mine / diag
    rz0 = dot(mine, precond)
    image = back / total_rows + damping * precond
    alpha0 = rz0 / dot(precond, image)
    resid = mine - alpha0 * image
    precond1 = resid / diag
    search = precond1 + dot(resid, precond1) / rz0 * precond
    out[...] = jnp.broadcast_to(search.astype(bf16)[None], out.shape)


def column(total_rows, parts, diag, mine):
    return pl.pallas_call(
        functools.partial(column_kernel, total_rows),
        out_shape=jax.ShapeDtypeStruct(parts.shape, bf16),
        compiler_params=pltpu.CompilerParams(vmem_limit_bytes=VMEM_BYTES),
        name="column",
    )(parts, diag, mine)


def second_kernel(*refs):
    low, high = refs[0:4], refs[4:8]
    message, rhs, prod_low, prod_high, stats, wide, direction = refs[8:]
    step = pl.program_id(0)

    @pl.when(step == 0)
    def _():
        count = rhs.shape[1] // LANES
        tests = rhs.shape[0]
        wide[...] = message[...].astype(f32)
        along = jnp.zeros((LANES, tests), f32)
        norm = jnp.zeros((LANES, tests), f32)
        for j in range(count):
            piece = wide[pl.ds(j, tests, stride=count), :].T
            along += piece * rhs[:, j * LANES:(j + 1) * LANES].astype(f32).T
            norm += piece * piece
            direction[j * LANES:(j + 1) * LANES, :] = piece.astype(bf16)
        stats[...] = jnp.zeros_like(stats)
        stats[1:2, :] = jnp.sum(along, axis=0, keepdims=True)
        stats[2:3, :] = jnp.sum(norm, axis=0, keepdims=True)

    for parts, prod in ((low, prod_low), (high, prod_high)):
        value = times(parts, direction)
        prod[...] = value
        stats[0:1, :] += jnp.sum(value * value, axis=0, keepdims=True)


def second(low, high, message, rhs):
    rows, block = low[0].shape
    tests, width = rhs.shape
    tile = pl.BlockSpec((TILE, block), lambda i: (i, 0))
    out = pl.BlockSpec((TILE, tests), lambda i: (i, 0))
    whole = lambda *shape: pl.BlockSpec(shape, lambda i: (0, 0))
    return pl.pallas_call(
        second_kernel,
        grid=(rows // TILE,),
        in_specs=[tile] * 8 + [whole(*message.shape), whole(tests, width)],
        out_specs=[out, out, whole(8, tests)],
        out_shape=[
            jax.ShapeDtypeStruct((rows, tests), f32),
            jax.ShapeDtypeStruct((rows, tests), f32),
            jax.ShapeDtypeStruct((8, tests), f32),
        ],
        scratch_shapes=[pltpu.VMEM(message.shape, f32), pltpu.VMEM((width, tests), bf16)],
        compiler_params=pltpu.CompilerParams(vmem_limit_bytes=VMEM_BYTES),
        cost_estimate=pl.CostEstimate(flops=4 * rows * width * tests, bytes_accessed=4 * rows * width, transcendentals=0),
        name="second",
    )(*low, *high, message, rhs)


def last_kernel(total_rows, scale, norms, start, stats, a_low, a_high, b_low, b_high, out):
    members = norms.shape[0] // 2
    norm0 = jnp.sum(norms[pl.ds(0, members, stride=2), :], axis=0, keepdims=True)
    norm1 = jnp.sum(norms[pl.ds(1, members, stride=2), :], axis=0, keepdims=True)
    alpha0 = start[0:1, :] / (norm0 / total_rows + damping * start[1:2, :])
    alpha1 = stats[1:2, :] / (norm1 / total_rows + damping * stats[2:3, :])
    alpha0, alpha1 = alpha0 * scale, alpha1 * scale
    half = a_low.shape[0]
    out[0:half, :] = (alpha0 * a_low[...] + alpha1 * b_low[...]).astype(bf16)
    out[half:, :] = (alpha0 * a_high[...] + alpha1 * b_high[...]).astype(bf16)


def last(total_rows, scale, norms, start, stats, prod0, prod1):
    half, tests = prod0[0].shape
    return pl.pallas_call(
        functools.partial(last_kernel, total_rows, scale),
        out_shape=jax.ShapeDtypeStruct((2 * half, tests), bf16),
        compiler_params=pltpu.CompilerParams(vmem_limit_bytes=VMEM_BYTES),
        name="last",
    )(norms, start, stats, *prod0, *prod1)


def local(train_feats, test_feats):
    rows, block = train_feats.shape
    tests, width = test_feats.shape
    feats = lax.axis_size("feat")
    members = lax.axis_size("train")
    total_rows = rows * members
    half = rows // 2
    count = width // LANES
    me = lax.axis_index("feat")
    owner = lax.axis_index("train")
    right, left = ring(feats, 1), ring(feats, -1)

    low, high = lax.optimization_barrier((train_feats[:half], train_feats[half:]))
    prev_low = lax.ppermute(low, "feat", right)
    next_high = lax.ppermute(high, "feat", left)
    prev_high = lax.ppermute(high, "feat", right)
    next_low = lax.ppermute(low, "feat", left)

    order = [me, (me + feats - 1) % feats, (me + 1) % feats, (me + 2) % feats]
    energy = jnp.sum(jnp.square(low.astype(f32)), axis=0) + jnp.sum(jnp.square(high.astype(f32)), axis=0)
    energy = jnp.sum(everyone(energy.reshape(block // LANES, LANES), "train", members), axis=0)
    energy, prev_low, next_high = lax.optimization_barrier((energy, prev_low, next_high))
    far_low = lax.ppermute(prev_low, "feat", right)
    far_high = lax.ppermute(next_high, "feat", left)
    energy = everyone(energy, "feat", feats)
    diag = jnp.concatenate([lax.dynamic_index_in_dim(energy, o, 0, False) for o in order], 0)
    diag = diag / total_rows + damping
    rhs = jnp.concatenate([lax.dynamic_slice_in_dim(test_feats, o * block, block, 1) for o in order], 1)
    wide = rhs.astype(f32)
    search = wide / diag.reshape(1, width)
    start = jnp.stack([jnp.sum(wide * search, axis=1), jnp.sum(search * search, axis=1)])
    direction = search.astype(bf16).T
    mine = lax.dynamic_index_in_dim(rhs, owner, 0, False).astype(f32).reshape(count, LANES)

    lows = (low, prev_low, next_low, far_low)
    highs = (high, prev_high, next_high, far_high)
    back, *prod0, norm0 = first(lows, highs, direction)
    back = lax.all_to_all(back.reshape(tests, count, LANES), "train", 0, 0, tiled=True)
    message = column(total_rows, back, diag, mine)
    message = lax.all_to_all(message, "train", 0, 0, tiled=True)
    *prod1, stats = second(lows, highs, message.reshape(tests * count, LANES), rhs)
    norms = everyone(jnp.concatenate([norm0, stats[0:1]], 0), "train", members)
    scale = 1.0 / float(width) ** 0.5
    return last(total_rows, scale, norms.reshape(2 * members, tests), start, stats, prod0, prod1)


def solution(mesh):
    return jax.shard_map(
        local,
        mesh=mesh,
        in_specs=(P("train", "feat"), P("feat", None)),
        out_specs=P("train", "feat"),
        check_vma=False,
    )
```

time: 789 us -> 184 us (0.23)
  waiting for transfers between devices: 482 us -> 67.2 us
  blocking collectives: 252 us -> 25.8 us
  starting transfers between devices: 0.26 us -> 61.5 us
  matrix products: 28.3 us -> 0 us
  Pallas kernels: 0 us -> 14.5 us
  between operations: 13.2 us -> 0.28 us
  local copies, waits for them, and re-layouts: 1.01 us -> 12.1 us
  other arithmetic: 10.3 us -> 1.86 us
    psum x2 -> x0, waiting for transfers between devices: 385 us -> none  [local(): image = lax.psum(back, 'train') / total_rows + damping * search]
    psum x1 -> x0, blocking collectives: 252 us -> none  [local(): lax.psum(jnp.sum(jnp.square(whole.astype(jnp.float32)), axis=0), 'train')]
    all_gather x1 -> x0, waiting for transfers between devices: 96.1 us -> none  [local(): whole = lax.all_gather(train_feats, 'feat', axis=1, tiled=True)]
    all_to_all x0 -> x4, waiting for transfers between devices: none -> 47.2 us  [the longest x3 26.7 us: everyone(): lax.all_to_all(jnp.broadcast_to(value[None], (count,) + value.shape), axi...]
    all_to_all x0 -> x4, starting transfers between devices: none -> 42.5 us  [the longest x3 27 us: everyone(): lax.all_to_all(jnp.broadcast_to(value[None], (count,) + value.shape), axi...]
    dot_general x3 -> x0, matrix products: 28.3 us -> none  [the longest x2 21.9 us: local(): jnp.einsum('np,nm->pm', whole, prod.astype(jnp.bfloat16), preferred_eleme...]
    all_to_all x0 -> x1, blocking collectives: none -> 25.8 us  [local(): message = lax.all_to_all(message, 'train', 0, 0, tiled=True)]
    ppermute x0 -> x6, waiting for transfers between devices: none -> 19.9 us  [the longest x1 19.9 us: local(): far_low = lax.ppermute(prev_low, 'feat', right)]
  transfers between devices with their start and end apart: 3 -> 10, of which waited for: 3 -> 5; matrix products, arithmetic and copies ran while one was open for 0% -> 2% of each run, Pallas kernels for 0% -> 0%
where the time goes in v2:
time: 184 us; the launch traced here: 183 us
  waiting for transfers between devices  67.2 us (37%)
  starting transfers between devices  61.5 us (33%)
  blocking collectives  25.8 us (14%)
  Pallas kernels  14.5 us (8%)
  local copies, waits for them, and re-layouts  12.1 us (7%)
  other arithmetic  1.86 us (1%)
    all_to_all x3, starting transfers between devices, everyone(): lax.all_to_all(jnp.broadcast_to(value[None], (count,) + value.shape), axi...  27 us
    all_to_all x3, waiting for transfers between devices, everyone(): lax.all_to_all(jnp.broadcast_to(value[None], (count,) + value.shape), axi...  26.7 us
    all_to_all x1, blocking collectives, local(): message = lax.all_to_all(message, 'train', 0, 0, tiled=True)  25.8 us
    all_to_all x1, waiting for transfers between devices, local(): lax.all_to_all(back.reshape(tests, count, LANES), 'train', 0, 0, tiled=True)  20.6 us
    ppermute x1, waiting for transfers between devices, local(): far_low = lax.ppermute(prev_low, 'feat', right)  19.9 us
    all_to_all x1, starting transfers between devices, local(): lax.all_to_all(back.reshape(tests, count, LANES), 'train', 0, 0, tiled=True)  15.5 us
    pallas_call x1, Pallas kernels, first(): pl.pallas_call(first_kernel, grid=(rows // TILE,), in_specs=[tile] * 8 +...  7.54 us
    unnamed x20, local copies, waits for them, and re-layouts  7.08 us
  transfers between devices with their start and end apart: 10, of which 5 were waited for; matrix products, arithmetic and copies ran while one was open for 2% of the time, Pallas kernels for 0%

profile of v2, /device:TPU:1, one launch (start us, length us, event | category | flops | bytes accessed | tf_op | source)
XLA Modules:
  0.0 183.3 jit_solution(16213712652560620395)
XLA Ops:
  0.0 1.7 fusion.9
  1.7 4.1 %collective-permute-start = (bf16[1024,512]{1,0:T(8,128)(2,1)S(1)}, bf16[1024,512]{1,0:T(8,128)(2,1)}, u32[]{:S(2)}, u32[]{:S(2)}) collective-permute-start(bf16[1024,512]{1,0:T(8,128)(2,1)S(1)} %get-tuple-element.17.refs_0_), channel_id=1, source_target_pairs={{0,1},{1,2},{2,3},{3,0},{4,5},{5,6},{6,7},{7,4},{8,9},{9,10},{10,1... | collective-permute-start | bytes 3145736 | tf_op jit(solution)/shard_map/ppermute | solution.py:199
  5.8 3.2 %collective-permute-start.1 = (bf16[1024,512]{1,0:T(8,128)(2,1)S(1)}, bf16[1024,512]{1,0:T(8,128)(2,1)}, u32[]{:S(2)}, u32[]{:S(2)}) collective-permute-start(bf16[1024,512]{1,0:T(8,128)(2,1)S(1)} %get-tuple-element.18.refs_4_), channel_id=1, source_target_pairs={{0,3},{1,0},{2,1},{3,2},{4,7},{5,4},{6,5},{7,6},{8,11},{9,8},{10,9... | collective-permute-start | bytes 3145736 | tf_op jit(solution)/shard_map/ppermute | solution.py:200
  10.2 18.3 %all-to-all-start = ((f32[128,4,128]{2,1,0:T(4,128)}), f32[128,4,128]{2,1,0:T(4,128)S(1)}, u32[]{:S(2)}, u32[]{:S(2)}) async-start(f32[128,4,128]{2,1,0:T(4,128)} %broadcast_in_dim.6), calls=%async_computation | async-start | bytes 524288 | tf_op jit(solution)/shard_map/all_to_all | solution.py:23
  28.5 3.2 %collective-permute-start.2 = (bf16[1024,512]{1,0:T(8,128)(2,1)S(1)}, bf16[1024,512]{1,0:T(8,128)(2,1)}, u32[]{:S(2)}, u32[]{:S(2)}) collective-permute-start(bf16[1024,512]{1,0:T(8,128)(2,1)S(1)} %get-tuple-element.17.refs_0_), channel_id=1, source_target_pairs={{0,3},{1,0},{2,1},{3,2},{4,7},{5,4},{6,5},{7,6},{8,11},{9,8},{10,9... | collective-permute-start | bytes 3145736 | tf_op jit(solution)/shard_map/ppermute | solution.py:202
  31.7 2.1 %collective-permute-start.4 = (bf16[1024,512]{1,0:T(8,128)(2,1)S(1)}, bf16[1024,512]{1,0:T(8,128)(2,1)}, u32[]{:S(2)}, u32[]{:S(2)}) collective-permute-start(bf16[1024,512]{1,0:T(8,128)(2,1)S(1)} %get-tuple-element.18.refs_4_), channel_id=1, source_target_pairs={{0,1},{1,2},{2,3},{3,0},{4,5},{5,6},{6,7},{7,4},{8,9},{9,10},{10,1... | collective-permute-start | bytes 3145736 | tf_op jit(solution)/shard_map/ppermute | solution.py:201
  33.9 9.9 %all-to-all-done = f32[128,4,128]{2,1,0:T(4,128)S(1)} async-done(((f32[128,4,128]{2,1,0:T(4,128)}), f32[128,4,128]{2,1,0:T(4,128)S(1)}, u32[]{:S(2)}, u32[]{:S(2)}) %all-to-all-start) | async-done | bytes 262176 | tf_op jit(solution)/shard_map/all_to_all | solution.py:23
  44.5 3.2 %all-to-all-start.1 = ((f32[4,4,128]{2,1,0:T(4,128)}), f32[4,4,128]{2,1,0:T(4,128)S(1)}, u32[]{:S(2)}, u32[]{:S(2)}) async-start(f32[4,4,128]{2,1,0:T(4,128)} %broadcast_in_dim.7), calls=%async_computation.1 | async-start | bytes 16384 | tf_op jit(solution)/shard_map/all_to_all | solution.py:23
  47.8 3.3 %collective-permute-start.3 = (bf16[1024,512]{1,0:T(8,128)(2,1)}, bf16[1024,512]{1,0:T(8,128)(2,1)}, u32[]{:S(2)}, u32[]{:S(2)}) collective-permute-start(bf16[1024,512]{1,0:T(8,128)(2,1)} %collective-permute-done.refs_1_), channel_id=1, source_target_pairs={{0,1},{1,2},{2,3},{3,0},{4,5},{5,6},{6,7},{7,4},{8,9},{9,10},{10,1... | collective-permute-start | bytes 3145736 | tf_op jit(solution)/shard_map/ppermute | solution.py:208
  51.1 3.2 %collective-permute-start.5 = (bf16[1024,512]{1,0:T(8,128)(2,1)}, bf16[1024,512]{1,0:T(8,128)(2,1)}, u32[]{:S(2)}, u32[]{:S(2)}) collective-permute-start(bf16[1024,512]{1,0:T(8,128)(2,1)} %collective-permute-done.1.refs_6_), channel_id=1, source_target_pairs={{0,3},{1,0},{2,1},{3,2},{4,7},{5,4},{6,5},{7,6},{8,11},{9,8},{10,9... | collective-permute-start | bytes 3145736 | tf_op jit(solution)/shard_map/ppermute | solution.py:209
  54.4 4.1 %all-to-all-done.1 = f32[4,4,128]{2,1,0:T(4,128)S(1)} async-done(((f32[4,4,128]{2,1,0:T(4,128)}), f32[4,4,128]{2,1,0:T(4,128)S(1)}, u32[]{:S(2)}, u32[]{:S(2)}) %all-to-all-start.1) | async-done | bytes 8224 | tf_op jit(solution)/shard_map/all_to_all | solution.py:23
  59.7 1.3 copy.6.refs_8_
  61.0 19.9 %collective-permute-done.3.refs_3_ = bf16[1024,512]{1,0:T(8,128)(2,1)} collective-permute-done((bf16[1024,512]{1,0:T(8,128)(2,1)}, bf16[1024,512]{1,0:T(8,128)(2,1)}, u32[]{:S(2)}, u32[]{:S(2)}) %collective-permute-start.3) | collective-permute-done | bytes 1048608 | tf_op jit(solution)/shard_map/ppermute | solution.py:208
  80.9 7.5 %first.1 = (bf16[2048,128]{1,0:T(8,128)(2,1)S(1)}, f32[1024,128]{1,0:T(8,128)S(1)}, f32[1024,128]{1,0:T(8,128)S(1)}, f32[1,128]{1,0:T(1,128)S(1)}) custom-call(bf16[1024,512]{1,0:T(8,128)(2,1)S(1)} %get-tuple-element.17.refs_0_, bf16[1024,512]{1,0:T(8,128)(2,1)} %collective-permute-done.refs_1_, bf16[1024,512]{1,0:T(8,128)(2,1)} %collective-permute-done.2.refs_2_, ...), custom_call_target="tpu_custom_call" | custom-call | flops 2147483648 | bytes 8388608 | tf_op jit(solution)/shard_map/first/pallas_call | solution.py:70
  90.9 15.5 %all-to-all-start.2 = ((bf16[128,16,128]{2,1,0:T(8,128)(2,1)}), bf16[128,16,128]{2,1,0:T(8,128)(2,1)S(1)}, u32[]{:S(2)}, u32[]{:S(2)}) async-start(bf16[128,16,128]{2,1,0:T(8,128)(2,1)} %bitcast.22), calls=%async_computation.2 | async-start | bytes 1048576 | tf_op jit(solution)/shard_map/all_to_all | solution.py:223
  106.4 20.6 %all-to-all-done.2.parts = bf16[128,16,128]{2,1,0:T(8,128)(2,1)S(1)} async-done(((bf16[128,16,128]{2,1,0:T(8,128)(2,1)}), bf16[128,16,128]{2,1,0:T(8,128)(2,1)S(1)}, u32[]{:S(2)}, u32[]{:S(2)}) %all-to-all-start.2) | async-done | bytes 524320 | tf_op jit(solution)/shard_map/all_to_all | solution.py:223
  127.3 25.8 %all_to_all.25 = bf16[128,16,128]{2,1,0:T(8,128)(2,1)S(1)} all-to-all(bf16[128,16,128]{2,1,0:T(8,128)(2,1)S(1)} %column.1), channel_id=1, replica_groups=mesh['train'=128,'feat'=4] {'train'}, dimensions={0} | all-to-all | bytes 1048576 | tf_op jit(solution)/shard_map/all_to_all | solution.py:225
  153.1 5.6 %second.1 = (f32[1024,128]{1,0:T(8,128)S(1)}, f32[1024,128]{1,0:T(8,128)S(1)}, f32[8,128]{1,0:T(8,128)S(1)}) custom-call(bf16[1024,512]{1,0:T(8,128)(2,1)S(1)} %get-tuple-element.17.refs_0_, bf16[1024,512]{1,0:T(8,128)(2,1)} %collective-permute-done.refs_1_, bf16[1024,512]{1,0:T(8,128)(2,1)} %collective-permute-done.2.refs_2_, ...), custom_call_target="tpu_custom_call" | custom-call | flops 1073741824 | bytes 8388608 | tf_op jit(solution)/shard_map/second/pallas_call | solution.py:147
  161.0 5.4 %all-to-all-start.4 = ((f32[128,2,128]{2,1,0:T(2,128)}), f32[128,2,128]{2,1,0:T(2,128)S(1)}, u32[]{:S(2)}, u32[]{:S(2)}) async-start(f32[128,2,128]{2,1,0:T(2,128)} %broadcast_in_dim.8), calls=%async_computation.4 | async-start | bytes 262144 | tf_op jit(solution)/shard_map/all_to_all | solution.py:23
  166.4 12.7 %all-to-all-done.4 = f32[128,2,128]{2,1,0:T(2,128)S(1)} async-done(((f32[128,2,128]{2,1,0:T(2,128)}), f32[128,2,128]{2,1,0:T(2,128)S(1)}, u32[]{:S(2)}, u32[]{:S(2)}) %all-to-all-start.4) | async-done | bytes 131104 | tf_op jit(solution)/shard_map/all_to_all | solution.py:23
  179.2 1.0 copy-done.3
  180.2 1.0 copy-done.5
  181.3 1.0 copy-done.7
  182.3 1.0 last.1
  (38 shorter events, 8.3 us)
Async XLA Ops:
  1.7 52.6 %copy-start.9 = (bf16[128,2048]{1,0:T(8,128)(2,1)S(1)}, bf16[128,2048]{1,0:T(8,128)(2,1)}, u32[]{:S(2)}) copy-start(bf16[128,2048]{1,0:T(8,128)(2,1)} %param.3) | copy-start | bytes 1572868
  1.7 42.2 %collective-permute-start = (bf16[1024,512]{1,0:T(8,128)(2,1)S(1)}, bf16[1024,512]{1,0:T(8,128)(2,1)}, u32[]{:S(2)}, u32[]{:S(2)}) collective-permute-start(bf16[1024,512]{1,0:T(8,128)(2,1)S(1)} %get-tuple-element.17.refs_0_), channel_id=1, source_target_pairs={{0,1},{1,2},{2,3},{3,0},{4,5},{5,6},{6,7},{7,4},{8,9},{9,10},{10,1... | collective-permute-start | bytes 3145736 | tf_op jit(solution)/shard_map/ppermute | solution.py:199
  5.8 38.1 %collective-permute-start.1 = (bf16[1024,512]{1,0:T(8,128)(2,1)S(1)}, bf16[1024,512]{1,0:T(8,128)(2,1)}, u32[]{:S(2)}, u32[]{:S(2)}) collective-permute-start(bf16[1024,512]{1,0:T(8,128)(2,1)S(1)} %get-tuple-element.18.refs_4_), channel_id=1, source_target_pairs={{0,3},{1,0},{2,1},{3,2},{4,7},{5,4},{6,5},{7,6},{8,11},{9,8},{10,9... | collective-permute-start | bytes 3145736 | tf_op jit(solution)/shard_map/ppermute | solution.py:200
  10.2 33.6 %all-to-all-start = ((f32[128,4,128]{2,1,0:T(4,128)}), f32[128,4,128]{2,1,0:T(4,128)S(1)}, u32[]{:S(2)}, u32[]{:S(2)}) async-start(f32[128,4,128]{2,1,0:T(4,128)} %broadcast_in_dim.6), calls=%async_computation | async-start | bytes 524288 | tf_op jit(solution)/shard_map/all_to_all | solution.py:23
  28.5 32.5 %collective-permute-start.2 = (bf16[1024,512]{1,0:T(8,128)(2,1)S(1)}, bf16[1024,512]{1,0:T(8,128)(2,1)}, u32[]{:S(2)}, u32[]{:S(2)}) collective-permute-start(bf16[1024,512]{1,0:T(8,128)(2,1)S(1)} %get-tuple-element.17.refs_0_), channel_id=1, source_target_pairs={{0,3},{1,0},{2,1},{3,2},{4,7},{5,4},{6,5},{7,6},{8,11},{9,8},{10,9... | collective-permute-start | bytes 3145736 | tf_op jit(solution)/shard_map/ppermute | solution.py:202
  31.7 29.3 %collective-permute-start.4 = (bf16[1024,512]{1,0:T(8,128)(2,1)S(1)}, bf16[1024,512]{1,0:T(8,128)(2,1)}, u32[]{:S(2)}, u32[]{:S(2)}) collective-permute-start(bf16[1024,512]{1,0:T(8,128)(2,1)S(1)} %get-tuple-element.18.refs_4_), channel_id=1, source_target_pairs={{0,1},{1,2},{2,3},{3,0},{4,5},{5,6},{6,7},{7,4},{8,9},{9,10},{10,1... | collective-permute-start | bytes 3145736 | tf_op jit(solution)/shard_map/ppermute | solution.py:201
  44.5 13.9 %all-to-all-start.1 = ((f32[4,4,128]{2,1,0:T(4,128)}), f32[4,4,128]{2,1,0:T(4,128)S(1)}, u32[]{:S(2)}, u32[]{:S(2)}) async-start(f32[4,4,128]{2,1,0:T(4,128)} %broadcast_in_dim.7), calls=%async_computation.1 | async-start | bytes 16384 | tf_op jit(solution)/shard_map/all_to_all | solution.py:23
  47.8 33.2 %collective-permute-start.3 = (bf16[1024,512]{1,0:T(8,128)(2,1)}, bf16[1024,512]{1,0:T(8,128)(2,1)}, u32[]{:S(2)}, u32[]{:S(2)}) collective-permute-start(bf16[1024,512]{1,0:T(8,128)(2,1)} %collective-permute-done.refs_1_), channel_id=1, source_target_pairs={{0,1},{1,2},{2,3},{3,0},{4,5},{5,6},{6,7},{7,4},{8,9},{9,10},{10,1... | collective-permute-start | bytes 3145736 | tf_op jit(solution)/shard_map/ppermute | solution.py:208
  51.1 29.8 %collective-permute-start.5 = (bf16[1024,512]{1,0:T(8,128)(2,1)}, bf16[1024,512]{1,0:T(8,128)(2,1)}, u32[]{:S(2)}, u32[]{:S(2)}) collective-permute-start(bf16[1024,512]{1,0:T(8,128)(2,1)} %collective-permute-done.1.refs_6_), channel_id=1, source_target_pairs={{0,3},{1,0},{2,1},{3,2},{4,7},{5,4},{6,5},{7,6},{8,11},{9,8},{10,9... | collective-permute-start | bytes 3145736 | tf_op jit(solution)/shard_map/ppermute | solution.py:209
  88.5 0.8 copy-start
  89.3 0.8 copy-start.2
  90.1 0.8 copy-start.8
  90.9 36.0 %all-to-all-start.2 = ((bf16[128,16,128]{2,1,0:T(8,128)(2,1)}), bf16[128,16,128]{2,1,0:T(8,128)(2,1)S(1)}, u32[]{:S(2)}, u32[]{:S(2)}) async-start(bf16[128,16,128]{2,1,0:T(8,128)(2,1)} %bitcast.22), calls=%async_computation.2 | async-start | bytes 1048576 | tf_op jit(solution)/shard_map/all_to_all | solution.py:223
  153.1 26.1 %copy-start.1 = (f32[1024,128]{1,0:T(8,128)S(1)}, f32[1024,128]{1,0:T(8,128)}, u32[]{:S(2)}) copy-start(f32[1024,128]{1,0:T(8,128)} %copy-done) | copy-start | bytes 1572868
  158.7 0.8 copy-start.4
  159.5 0.8 copy-start.6
  161.0 18.1 %all-to-all-start.4 = ((f32[128,2,128]{2,1,0:T(2,128)}), f32[128,2,128]{2,1,0:T(2,128)S(1)}, u32[]{:S(2)}, u32[]{:S(2)}) async-start(f32[128,2,128]{2,1,0:T(2,128)} %broadcast_in_dim.8), calls=%async_computation.4 | async-start | bytes 262144 | tf_op jit(solution)/shard_map/all_to_all | solution.py:23
  179.2 1.0 copy-start.3
  180.2 1.0 copy-start.5
  181.2 1.0 copy-start.7

commit v3 on v2

v3 whole, which is shorter than its diff:
```python
import functools

import jax
import jax.numpy as jnp
from jax import lax
from jax.experimental import pallas as pl
from jax.experimental.pallas import tpu as pltpu
from jax.sharding import PartitionSpec as P

damping = 0.05
bf16 = jnp.bfloat16
f32 = jnp.float32
LANES = 128
TILE = 256
EARLY = 768
VMEM_BYTES = 20 * 1024 * 1024


def ring(size, step):
    return [(i, (i + step) % size) for i in range(size)]


def everyone(value, axis, count):
    return lax.all_to_all(jnp.broadcast_to(value[None], (count,) + value.shape), axis, 0, 0, tiled=True)


def times(parts, direction_ref):
    total = None
    for i, part in enumerate(parts):
        block = part.shape[1]
        term = jnp.dot(part[...], direction_ref[i * block:(i + 1) * block, :], preferred_element_type=f32)
        total = term if total is None else total + term
    return total


def partial_kernel(*refs):
    low, high = refs[0:3], refs[3:6]
    direction, out_low, out_high = refs[6:]
    out_low[...] = times(low, direction)
    out_high[...] = times(high, direction)


def partial(low, high, direction):
    rows, block = low[0].shape
    width, tests = direction.shape
    tile = pl.BlockSpec((TILE, block), lambda i: (i, 0))
    out = pl.BlockSpec((TILE, tests), lambda i: (i, 0))
    return pl.pallas_call(
        partial_kernel,
        grid=(rows // TILE,),
        in_specs=[tile] * 6 + [pl.BlockSpec((width, tests), lambda i: (0, 0))],
        out_specs=[out, out],
        out_shape=[jax.ShapeDtypeStruct((rows, tests), f32)] * 2,
        compiler_params=pltpu.CompilerParams(vmem_limit_bytes=VMEM_BYTES),
        cost_estimate=pl.CostEstimate(flops=3 * rows * width * tests, bytes_accessed=3 * rows * width, transcendentals=0),
        name="partial",
    )(*low, *high, direction)


def first_kernel(final, *refs):
    low, high = refs[0:4], refs[4:8]
    direction, part_low, part_high, total_in, norm_in = refs[8:13]
    if final:
        back, norm, prod_low, prod_high, total, spread = refs[13:]
    else:
        total, norm, prod_low, prod_high = refs[13:]
    step = pl.program_id(0)

    @pl.when(step == 0)
    def _():
        total[...] = total_in[...]
        norm[...] = norm_in[...]

    block = low[0].shape[1]
    for parts, part, prod in ((low, part_low, prod_low), (high, part_high, prod_high)):
        value = part[...] + jnp.dot(parts[3][...], direction[3 * block:, :], preferred_element_type=f32)
        prod[...] = value
        norm[...] += jnp.sum(value * value, axis=0, keepdims=True)
        turned = value.T.astype(bf16)
        for i, tile in enumerate(parts):
            total[:, i * block:(i + 1) * block] += jnp.dot(turned, tile[...], preferred_element_type=f32)

    if final:
        @pl.when(step == pl.num_programs(0) - 1)
        def _():
            count = total.shape[1] // LANES
            tests = total.shape[0]
            for j in range(count):
                spread[pl.ds(j, tests, stride=count), :] = total[:, j * LANES:(j + 1) * LANES]
            back[...] = spread[...].astype(bf16)


def first(final, low, high, direction, part, total, norm, base):
    rows, block = low[3].shape
    width, tests = direction.shape
    skip = base // TILE
    shifted = pl.BlockSpec((TILE, block), lambda i: (i + skip, 0))
    own = pl.BlockSpec((TILE, block), lambda i: (i, 0))
    taken = pl.BlockSpec((TILE, tests), lambda i: (i + skip, 0))
    out = pl.BlockSpec((TILE, tests), lambda i: (i, 0))
    whole = lambda *shape: pl.BlockSpec(shape, lambda i: (0, 0))
    count = width // LANES
    sums = (tests * count, LANES) if final else (tests, width)
    return pl.pallas_call(
        functools.partial(first_kernel, final),
        grid=(rows // TILE,),
        in_specs=[shifted, shifted, shifted, own] * 2 + [whole(width, tests), taken, taken, whole(tests, width), whole(1, tests)],
        out_specs=[whole(*sums), whole(1, tests), out, out],
        out_shape=[
            jax.ShapeDtypeStruct(sums, bf16 if final else f32),
            jax.ShapeDtypeStruct((1, tests), f32),
            jax.ShapeDtypeStruct((rows, tests), f32),
            jax.ShapeDtypeStruct((rows, tests), f32),
        ],
        scratch_shapes=[pltpu.VMEM((tests, width), f32), pltpu.VMEM((tests * count, LANES), f32)] if final else [],
        compiler_params=pltpu.CompilerParams(vmem_limit_bytes=VMEM_BYTES),
        cost_estimate=pl.CostEstimate(flops=5 * rows * width * tests, bytes_accessed=4 * rows * width, transcendentals=0),
        name="first",
    )(*low, *high, direction, *part, total, norm)


def column_kernel(total_rows, parts, diag_ref, mine_ref, out):
    diag, mine = diag_ref[...], mine_ref[...]

    def dot(a, b):
        return jnp.sum(jnp.sum(a * b, axis=0, keepdims=True), axis=1, keepdims=True)

    back = jnp.sum(parts[...].astype(f32), axis=0)
    precond = mine / diag
    rz0 = dot(mine, precond)
    image = back / total_rows + damping * precond
    alpha0 = rz0 / dot(precond, image)
    resid = mine - alpha0 * image
    precond1 = resid / diag
    search = precond1 + dot(resid, precond1) / rz0 * precond
    out[...] = jnp.broadcast_to(search.astype(bf16)[None], out.shape)


def column(total_rows, parts, diag, mine):
    return pl.pallas_call(
        functools.partial(column_kernel, total_rows),
        out_shape=jax.ShapeDtypeStruct(parts.shape, bf16),
        compiler_params=pltpu.CompilerParams(vmem_limit_bytes=VMEM_BYTES),
        name="column",
    )(parts, diag, mine)


def second_kernel(early, *refs):
    low, high = refs[0:3], refs[3:6]
    far = refs[6:10]
    message, rhs, norm0, prod_low, prod_high, stats, norms, wide, direction, norm1 = refs[10:]
    step = pl.program_id(0)
    block = low[0].shape[1]

    @pl.when(step == 0)
    def _():
        count = rhs.shape[1] // LANES
        tests = rhs.shape[0]
        wide[...] = message[...].astype(f32)
        along = jnp.zeros((LANES, tests), f32)
        norm = jnp.zeros((LANES, tests), f32)
        for j in range(count):
            piece = wide[pl.ds(j, tests, stride=count), :]
            along += piece * rhs[:, j * LANES:(j + 1) * LANES].astype(f32)
            norm += piece * piece
            direction[j * LANES:(j + 1) * LANES, :] = piece.T.astype(bf16)
        norm1[...] = jnp.zeros_like(norm1)
        stats[...] = jnp.zeros_like(stats)
        stats[0:1, :] = jnp.sum(along.T, axis=0, keepdims=True)
        stats[1:2, :] = jnp.sum(norm.T, axis=0, keepdims=True)

    for parts, one, two, prod in ((low, far[0], far[1], prod_low), (high, far[2], far[3], prod_high)):
        last = jnp.where(step < early, one[...], two[...])
        value = times(parts, direction) + jnp.dot(last, direction[3 * block:, :], preferred_element_type=f32)
        prod[...] = value
        norm1[...] += jnp.sum(value * value, axis=0, keepdims=True)

    @pl.when(step == pl.num_programs(0) - 1)
    def _():
        even = lax.broadcasted_iota(jnp.int32, norms.shape, 0) % 2 == 0
        norms[...] = jnp.where(even, norm0[...], norm1[...])


def second(low, high, far, message, rhs, norm0, members):
    rows, block = low[0].shape
    tests, width = rhs.shape
    early, late = far[0].shape[0] // TILE, far[1].shape[0] // TILE
    tile = pl.BlockSpec((TILE, block), lambda i: (i, 0))
    one = pl.BlockSpec((TILE, block), lambda i: (jnp.minimum(i, early - 1), 0))
    two = pl.BlockSpec((TILE, block), lambda i: (jnp.maximum(i - early, 0), 0))
    out = pl.BlockSpec((TILE, tests), lambda i: (i, 0))
    whole = lambda *shape: pl.BlockSpec(shape, lambda i: (0, 0))
    return pl.pallas_call(
        functools.partial(second_kernel, early),
        grid=(early + late,),
        in_specs=[tile] * 6 + [one, two, one, two] + [whole(*message.shape), whole(tests, width), whole(1, tests)],
        out_specs=[out, out, whole(8, tests), whole(2 * members, tests)],
        out_shape=[
            jax.ShapeDtypeStruct((rows, tests), f32),
            jax.ShapeDtypeStruct((rows, tests), f32),
            jax.ShapeDtypeStruct((8, tests), f32),
            jax.ShapeDtypeStruct((2 * members, tests), f32),
        ],
        scratch_shapes=[pltpu.VMEM(message.shape, f32), pltpu.VMEM((width, tests), bf16), pltpu.VMEM((1, tests), f32)],
        compiler_params=pltpu.CompilerParams(vmem_limit_bytes=VMEM_BYTES),
        cost_estimate=pl.CostEstimate(flops=4 * rows * width * tests, bytes_accessed=4 * rows * width, transcendentals=0),
        name="second",
    )(*low, *high, *far, message, rhs, norm0)


def last_kernel(total_rows, scale, early, norms, start, stats, *refs):
    a_low, a_high, b_low, b_high, c_low, c_high, out = refs
    members = norms.shape[0] // 2
    norm0 = jnp.sum(norms[pl.ds(0, members, stride=2), :], axis=0, keepdims=True)
    norm1 = jnp.sum(norms[pl.ds(1, members, stride=2), :], axis=0, keepdims=True)
    alpha0 = start[0:1, :] / (norm0 / total_rows + damping * start[1:2, :])
    alpha1 = stats[0:1, :] / (norm1 / total_rows + damping * stats[1:2, :])
    alpha0, alpha1 = alpha0 * scale, alpha1 * scale
    half = c_low.shape[0]
    for base, one, two, both in ((0, a_low, b_low, c_low), (half, a_high, b_high, c_high)):
        out[base:base + early, :] = (alpha0 * one[...] + alpha1 * both[0:early, :]).astype(bf16)
        out[base + early:base + half, :] = (alpha0 * two[...] + alpha1 * both[early:, :]).astype(bf16)


def last(total_rows, scale, norms, start, stats, early, late, prod1):
    half, tests = prod1[0].shape
    return pl.pallas_call(
        functools.partial(last_kernel, total_rows, scale, early[0].shape[0]),
        out_shape=jax.ShapeDtypeStruct((2 * half, tests), bf16),
        compiler_params=pltpu.CompilerParams(vmem_limit_bytes=VMEM_BYTES),
        name="last",
    )(norms, start, stats, *early, *late, *prod1)


def local(train_feats, test_feats):
    rows, block = train_feats.shape
    tests, width = test_feats.shape
    feats = lax.axis_size("feat")
    members = lax.axis_size("train")
    total_rows = rows * members
    half = rows // 2
    count = width // LANES
    me = lax.axis_index("feat")
    owner = lax.axis_index("train")
    right, left = ring(feats, 1), ring(feats, -1)

    low, high = lax.optimization_barrier((train_feats[:half], train_feats[half:]))
    prev_low = lax.ppermute(low, "feat", right)
    next_high = lax.ppermute(high, "feat", left)
    prev_high = lax.ppermute(high, "feat", right)
    next_low = lax.ppermute(low, "feat", left)

    order = [me, (me + feats - 1) % feats, (me + 1) % feats, (me + 2) % feats]
    energy = jnp.sum(jnp.square(low.astype(f32)), axis=0) + jnp.sum(jnp.square(high.astype(f32)), axis=0)
    energy = jnp.sum(everyone(energy.reshape(block // LANES, LANES), "train", members), axis=0)
    energy, prev_low, next_high = lax.optimization_barrier((energy, prev_low, next_high))
    far_low = lax.ppermute(prev_low[:EARLY], "feat", right)
    far_high = lax.ppermute(next_high[:EARLY], "feat", left)
    far_low2 = lax.ppermute(prev_low[EARLY:], "feat", right)
    far_high2 = lax.ppermute(next_high[EARLY:], "feat", left)
    energy = everyone(energy, "feat", feats)
    diag = jnp.concatenate([lax.dynamic_index_in_dim(energy, o, 0, False) for o in order], 0)
    diag = diag / total_rows + damping
    rhs = jnp.concatenate([lax.dynamic_slice_in_dim(test_feats, o * block, block, 1) for o in order], 1)
    wide = rhs.astype(f32)
    search = wide / diag.reshape(1, width)
    start = jnp.stack([jnp.sum(wide * search, axis=1), jnp.sum(search * search, axis=1)])
    direction = search.astype(bf16).T
    mine = lax.dynamic_index_in_dim(rhs, owner, 0, False).astype(f32).reshape(count, LANES)

    lows, highs = (low, prev_low, next_low), (high, prev_high, next_high)
    part = partial(lows, highs, direction)
    zeros = jnp.zeros((tests, width), f32), jnp.zeros((1, tests), f32)
    total, norm0, *early = first(False, (*lows, far_low), (*highs, far_high), direction, part, *zeros, 0)
    total, mine, start = lax.optimization_barrier((total, mine, start))
    back, norm0, *late = first(True, (*lows, far_low2), (*highs, far_high2), direction, part, total, norm0, EARLY)
    back = lax.all_to_all(back.reshape(tests, count, LANES), "train", 0, 0, tiled=True)
    message = column(total_rows, back, diag, mine)
    message = lax.all_to_all(message, "train", 0, 0, tiled=True)
    far = (far_low, far_low2, far_high, far_high2)
    *prod1, stats, norms = second(lows, highs, far, message.reshape(tests * count, LANES), rhs, norm0, members)
    norms = lax.all_to_all(norms.reshape(members, 2, tests), "train", 0, 0, tiled=True)
    scale = 1.0 / float(width) ** 0.5
    return last(total_rows, scale, norms.reshape(2 * members, tests), start, stats, early, late, prod1)


def solution(mesh):
    return jax.shard_map(
        local,
        mesh=mesh,
        in_specs=(P("train", "feat"), P("feat", None)),
        out_specs=P("train", "feat"),
        check_vma=False,
    )
```

time: 184 us -> 171 us (0.929)
  waiting for transfers between devices: 67.2 us -> 10.3 us
  blocking collectives: 25.8 us -> 76.6 us
  starting transfers between devices: 61.5 us -> 47 us
  Pallas kernels: 14.5 us -> 17.5 us
  local copies, waits for them, and re-layouts: 12.1 us -> 14.3 us
    all_to_all x0 -> x2, blocking collectives: none -> 50.8 us  [the longest x1 32.9 us: local(): lax.all_to_all(back.reshape(tests, count, LANES), 'train', 0, 0, tiled=True)]
    all_to_all x1 -> x0, waiting for transfers between devices: 20.6 us -> none  [local(): lax.all_to_all(back.reshape(tests, count, LANES), 'train', 0, 0, tiled=True)]
    ppermute x2 -> x4, waiting for transfers between devices: 19.9 us -> 0.42 us  [the longest x1 0.42 us: local(): far_high2 = lax.ppermute(next_high[EARLY:], 'feat', left)]
    all_to_all x3 -> x2, waiting for transfers between devices: 26.7 us -> 9.91 us  [everyone(): lax.all_to_all(jnp.broadcast_to(value[None], (count,) + value.shape), axi...]
    all_to_all x1 -> x0, starting transfers between devices: 15.5 us -> none  [local(): lax.all_to_all(back.reshape(tests, count, LANES), 'train', 0, 0, tiled=True)]
    ppermute x2 -> x4, starting transfers between devices: 6.5 us -> 13 us  [the longest x1 4.38 us: local(): far_high2 = lax.ppermute(next_high[EARLY:], 'feat', left)]
    all_to_all x3 -> x2, starting transfers between devices: 27 us -> 21.6 us  [everyone(): lax.all_to_all(jnp.broadcast_to(value[None], (count,) + value.shape), axi...]
    slice x1 -> x4, local copies, waits for them, and re-layouts: 0.01 us -> 5.41 us  [the longest x1 2.07 us: local(): far_high = lax.ppermute(next_high[:EARLY], 'feat', left)]
  transfers between devices with their start and end apart: 10 -> 10, of which waited for: 5 -> 2; matrix products, arithmetic and copies ran while one was open for 2% -> 8% of each run, Pallas kernels for 0% -> 5%
where the time goes in v3:
time: 171 us; the launch traced here: 170 us
  blocking collectives  76.6 us (45%)
  starting transfers between devices  47 us (27%)
  Pallas kernels  17.5 us (10%)
  local copies, waits for them, and re-layouts  14.3 us (8%)
  waiting for transfers between devices  10.3 us (6%)
  other arithmetic  3.62 us (2%)
    all_to_all x1, blocking collectives, local(): lax.all_to_all(back.reshape(tests, count, LANES), 'train', 0, 0, tiled=True)  32.9 us
    all_to_all x1, blocking collectives, local(): message = lax.all_to_all(message, 'train', 0, 0, tiled=True)  25.8 us
    all_to_all x2, starting transfers between devices, everyone(): lax.all_to_all(jnp.broadcast_to(value[None], (count,) + value.shape), axi...  21.6 us
    all_to_all x1, blocking collectives, local(): lax.all_to_all(norms.reshape(members, 2, tests), 'train', 0, 0, tiled=True)  17.9 us
    all_to_all x2, waiting for transfers between devices, everyone(): lax.all_to_all(jnp.broadcast_to(value[None], (count,) + value.shape), axi...  9.91 us
    pallas_call x2, Pallas kernels, first(): pl.pallas_call(functools.partial(first_kernel, final), grid=(rows // TILE...  6.76 us
    pallas_call x1, Pallas kernels, second(): pl.pallas_call(functools.partial(second_kernel, early), grid=(early + lat...  5.33 us
    ppermute x1, starting transfers between devices, local(): far_high2 = lax.ppermute(next_high[EARLY:], 'feat', left)  4.38 us
  transfers between devices with their start and end apart: 10, of which 2 were waited for; matrix products, arithmetic and copies ran while one was open for 8% of the time, Pallas kernels for 5%

profile of v3, /device:TPU:1, one launch (start us, length us, event | category | flops | bytes accessed | tf_op | source)
XLA Modules:
  0.0 169.6 jit_solution(15863054151165278959)
XLA Ops:
  0.0 1.7 fusion.9
  1.7 3.9 %collective-permute-start = (bf16[1024,512]{1,0:T(8,128)(2,1)S(1)}, bf16[1024,512]{1,0:T(8,128)(2,1)S(1)}, u32[]{:S(2)}, u32[]{:S(2)}) collective-permute-start(bf16[1024,512]{1,0:T(8,128)(2,1)S(1)} %get-tuple-element.27.refs_0_), channel_id=1, source_target_pairs={{0,1},{1,2},{2,3},{3,0},{4,5},{5,6},{6,7},{7,4},{8,9},{9,10},{10,1... | collective-permute-start | bytes 3145736 | tf_op jit(solution)/shard_map/ppermute | solution.py:248
  5.6 3.2 %collective-permute-start.1 = (bf16[1024,512]{1,0:T(8,128)(2,1)S(1)}, bf16[1024,512]{1,0:T(8,128)(2,1)}, u32[]{:S(2)}, u32[]{:S(2)}) collective-permute-start(bf16[1024,512]{1,0:T(8,128)(2,1)S(1)} %get-tuple-element.28.refs_3_.refs_4_), channel_id=1, source_target_pairs={{0,3},{1,0},{2,1},{3,2},{4,7},{5,4},{6,5},{7,6},{8,11},{9,8},{10,9... | collective-permute-start | bytes 3145736 | tf_op jit(solution)/shard_map/ppermute | solution.py:249
  10.0 18.3 %all-to-all-start = ((f32[128,4,128]{2,1,0:T(4,128)}), f32[128,4,128]{2,1,0:T(4,128)S(1)}, u32[]{:S(2)}, u32[]{:S(2)}) async-start(f32[128,4,128]{2,1,0:T(4,128)} %broadcast_in_dim.8), calls=%async_computation | async-start | bytes 524288 | tf_op jit(solution)/shard_map/all_to_all | solution.py:24
  28.4 3.2 %collective-permute-start.2 = (bf16[1024,512]{1,0:T(8,128)(2,1)S(1)}, bf16[1024,512]{1,0:T(8,128)(2,1)}, u32[]{:S(2)}, u32[]{:S(2)}) collective-permute-start(bf16[1024,512]{1,0:T(8,128)(2,1)S(1)} %get-tuple-element.27.refs_0_), channel_id=1, source_target_pairs={{0,3},{1,0},{2,1},{3,2},{4,7},{5,4},{6,5},{7,6},{8,11},{9,8},{10,9... | collective-permute-start | bytes 3145736 | tf_op jit(solution)/shard_map/ppermute | solution.py:251
  31.6 2.1 %collective-permute-start.3 = (bf16[1024,512]{1,0:T(8,128)(2,1)S(1)}, bf16[1024,512]{1,0:T(8,128)(2,1)}, u32[]{:S(2)}, u32[]{:S(2)}) collective-permute-start(bf16[1024,512]{1,0:T(8,128)(2,1)S(1)} %get-tuple-element.28.refs_3_.refs_4_), channel_id=1, source_target_pairs={{0,1},{1,2},{2,3},{3,0},{4,5},{5,6},{6,7},{7,4},{8,9},{9,10},{10,1... | collective-permute-start | bytes 3145736 | tf_op jit(solution)/shard_map/ppermute | solution.py:250
  33.7 9.9 %all-to-all-done = f32[128,4,128]{2,1,0:T(4,128)S(1)} async-done(((f32[128,4,128]{2,1,0:T(4,128)}), f32[128,4,128]{2,1,0:T(4,128)S(1)}, u32[]{:S(2)}, u32[]{:S(2)}) %all-to-all-start) | async-done | bytes 262176 | tf_op jit(solution)/shard_map/all_to_all | solution.py:24
  44.4 3.2 %all-to-all-start.1 = ((f32[4,4,128]{2,1,0:T(4,128)}), f32[4,4,128]{2,1,0:T(4,128)S(1)}, u32[]{:S(2)}, u32[]{:S(2)}) async-start(f32[4,4,128]{2,1,0:T(4,128)} %broadcast_in_dim.18), calls=%async_computation.1 | async-start | bytes 16384 | tf_op jit(solution)/shard_map/all_to_all | solution.py:24
  47.6 1.9 %constant_dynamic-slice_fusion.7 = (bf16[128,512]{1,0:T(8,128)(2,1)S(1)}, bf16[128,512]{1,0:T(8,128)(2,1)}, bf16[128,512]{1,0:T(8,128)(2,1)}, bf16[128,512]{1,0:T(8,128)(2,1)}) fusion(bf16[128,2048]{1,0:T(8,128)(2,1)} %param.3, s32[]{:T(128)S(6)} %select_n.44, s32[]{:T(128)S(6)} %select_n.46, s32[]{:T(128)S(6)} %select_n.50, s32[]{:T(128)S(6)} %select_n.48), kind=kLoop, calls=%fused_computation.19 | loop fusion | bytes 1048592 | tf_op jit(solution)/shard_map/dynamic_slice | solution.py:264
  51.2 2.1 %slice.22 = bf16[768,512]{1,0:T(8,128)(2,1)} slice(bf16[1024,512]{1,0:T(8,128)(2,1)} %collective-permute-done.1.refs_5_.refs_6_), slice={[0:768], [0:512]} | slice | bytes 1572864 | tf_op jit(solution)/shard_map/slice | solution.py:258
  53.2 1.7 slice.23
  54.9 3.3 %collective-permute-start.4 = (bf16[768,512]{1,0:T(8,128)(2,1)}, bf16[768,512]{1,0:T(8,128)(2,1)}, u32[]{:S(2)}, u32[]{:S(2)}) collective-permute-start(bf16[768,512]{1,0:T(8,128)(2,1)} %slice.20), channel_id=1, source_target_pairs={{0,1},{1,2},{2,3},{3,0},{4,5},{5,6},{6,7},{7,4},{8,9},{9,10},{10,1... | collective-permute-start | bytes 2359304 | tf_op jit(solution)/shard_map/ppermute | solution.py:257
  58.2 3.2 %collective-permute-start.6 = (bf16[768,512]{1,0:T(8,128)(2,1)}, bf16[768,512]{1,0:T(8,128)(2,1)}, u32[]{:S(2)}, u32[]{:S(2)}) collective-permute-start(bf16[768,512]{1,0:T(8,128)(2,1)} %slice.22), channel_id=1, source_target_pairs={{0,3},{1,0},{2,1},{3,2},{4,7},{5,4},{6,5},{7,6},{8,11},{9,8},{10,9... | collective-permute-start | bytes 2359304 | tf_op jit(solution)/shard_map/ppermute | solution.py:258
  61.4 2.1 %collective-permute-start.5 = (bf16[256,512]{1,0:T(8,128)(2,1)}, bf16[256,512]{1,0:T(8,128)(2,1)S(1)}, u32[]{:S(2)}, u32[]{:S(2)}) collective-permute-start(bf16[256,512]{1,0:T(8,128)(2,1)} %slice.21), channel_id=1, source_target_pairs={{0,1},{1,2},{2,3},{3,0},{4,5},{5,6},{6,7},{7,4},{8,9},{9,10},{10,1... | collective-permute-start | bytes 786440 | tf_op jit(solution)/shard_map/ppermute | solution.py:259
  63.6 1.3 fusion
  66.6 2.0 %copy.12.refs_6_.refs_8_ = bf16[2048,128]{1,0:T(8,128)(2,1)} copy(bf16[2048,128]{0,1:T(8,128)(2,1)} %fusion.2) | data formatting | bytes 1048576 | tf_op jit(solution)/shard_map/transpose | solution.py:268
  69.5 4.4 %collective-permute-start.7 = (bf16[256,512]{1,0:T(8,128)(2,1)}, bf16[256,512]{1,0:T(8,128)(2,1)S(1)}, u32[]{:S(2)}, u32[]{:S(2)}) collective-permute-start(bf16[256,512]{1,0:T(8,128)(2,1)} %slice.23), channel_id=1, source_target_pairs={{0,3},{1,0},{2,1},{3,2},{4,7},{5,4},{6,5},{7,6},{8,11},{9,8},{10,9... | collective-permute-start | bytes 786440 | tf_op jit(solution)/shard_map/ppermute | solution.py:260
  74.9 4.1 %partial.1 = (f32[1024,128]{1,0:T(8,128)S(1)}, f32[1024,128]{1,0:T(8,128)S(1)}) custom-call(bf16[1024,512]{1,0:T(8,128)(2,1)S(1)} %get-tuple-element.27.refs_0_, bf16[1024,512]{1,0:T(8,128)(2,1)S(1)} %collective-permute-done.refs_1_, bf16[1024,512]{1,0:T(8,128)(2,1)} %collective-permute-done.2.refs_2_, ...), custom_call_target="tpu_custom_call" | custom-call | flops 805306368 | bytes 6291456 | tf_op jit(solution)/shard_map/partial/pallas_call | solution.py:48
  79.1 4.5 %first.2 = (f32[128,2048]{1,0:T(8,128)S(1)}, f32[1,128]{1,0:T(1,128)S(1)}, f32[768,128]{1,0:T(8,128)S(1)}, f32[768,128]{1,0:T(8,128)S(1)}) custom-call(bf16[1024,512]{1,0:T(8,128)(2,1)S(1)} %get-tuple-element.27.refs_0_, bf16[1024,512]{1,0:T(8,128)(2,1)S(1)} %collective-permute-done.refs_1_, bf16[1024,512]{1,0:T(8,128)(2,1)} %collective-permute-done.2.refs_2_, ...), custom_call_target="tpu_custom_call" | custom-call | flops 1006632960 | bytes 6291456 | tf_op jit(solution)/shard_map/first/pallas_call | solution.py:104
  84.1 2.2 %first.3 = (bf16[2048,128]{1,0:T(8,128)(2,1)S(1)}, f32[1,128]{1,0:T(1,128)S(1)}, f32[256,128]{1,0:T(8,128)S(1)}, f32[256,128]{1,0:T(8,128)S(1)}) custom-call(bf16[1024,512]{1,0:T(8,128)(2,1)S(1)} %get-tuple-element.27.refs_0_, bf16[1024,512]{1,0:T(8,128)(2,1)S(1)} %collective-permute-done.refs_1_, bf16[1024,512]{1,0:T(8,128)(2,1)} %collective-permute-done.2.refs_2_, ...), custom_call_target="tpu_custom_call" | custom-call | flops 335544320 | bytes 2097152 | tf_op jit(solution)/shard_map/first/pallas_call | solution.py:104
  86.3 32.9 %all_to_all.25.parts = bf16[128,16,128]{2,1,0:T(8,128)(2,1)S(1)} all-to-all(bf16[128,16,128]{2,1,0:T(8,128)(2,1)S(1)} %bitcast.23), channel_id=1, replica_groups=mesh['train'=128,'feat'=4] {'train'}, dimensions={0} | all-to-all | bytes 1048576 | tf_op jit(solution)/shard_map/all_to_all | solution.py:277
  119.6 25.8 %all_to_all.26 = bf16[128,16,128]{2,1,0:T(8,128)(2,1)S(1)} all-to-all(bf16[128,16,128]{2,1,0:T(8,128)(2,1)S(1)} %column.1), channel_id=1, replica_groups=mesh['train'=128,'feat'=4] {'train'}, dimensions={0} | all-to-all | bytes 1048576 | tf_op jit(solution)/shard_map/all_to_all | solution.py:279
  145.3 5.3 %second.1 = (f32[1024,128]{1,0:T(8,128)S(1)}, f32[1024,128]{1,0:T(8,128)S(1)}, f32[8,128]{1,0:T(8,128)S(1)}, f32[256,128]{1,0:T(8,128)S(1)}) custom-call(bf16[1024,512]{1,0:T(8,128)(2,1)S(1)} %get-tuple-element.27.refs_0_, bf16[1024,512]{1,0:T(8,128)(2,1)S(1)} %collective-permute-done.refs_1_, bf16[1024,512]{1,0:T(8,128)(2,1)} %collective-permute-done.2.refs_2_, ...), custom_call_target="tpu_custom_call" | custom-call | flops 1073741824 | bytes 8388608 | tf_op jit(solution)/shard_map/second/pallas_call | solution.py:193
  150.7 17.9 %all_to_all.27 = f32[128,2,128]{2,1,0:T(2,128)S(1)} all-to-all(f32[128,2,128]{2,1,0:T(2,128)S(1)} %bitcast.24), channel_id=1, replica_groups=mesh['train'=128,'feat'=4] {'train'}, dimensions={0} | all-to-all | bytes 262144 | tf_op jit(solution)/shard_map/all_to_all | solution.py:282
  (31 shorter events, 9.0 us)
Async XLA Ops:
  1.7 42.1 %collective-permute-start = (bf16[1024,512]{1,0:T(8,128)(2,1)S(1)}, bf16[1024,512]{1,0:T(8,128)(2,1)S(1)}, u32[]{:S(2)}, u32[]{:S(2)}) collective-permute-start(bf16[1024,512]{1,0:T(8,128)(2,1)S(1)} %get-tuple-element.27.refs_0_), channel_id=1, source_target_pairs={{0,1},{1,2},{2,3},{3,0},{4,5},{5,6},{6,7},{7,4},{8,9},{9,10},{10,1... | collective-permute-start | bytes 3145736 | tf_op jit(solution)/shard_map/ppermute | solution.py:248
  5.6 38.1 %collective-permute-start.1 = (bf16[1024,512]{1,0:T(8,128)(2,1)S(1)}, bf16[1024,512]{1,0:T(8,128)(2,1)}, u32[]{:S(2)}, u32[]{:S(2)}) collective-permute-start(bf16[1024,512]{1,0:T(8,128)(2,1)S(1)} %get-tuple-element.28.refs_3_.refs_4_), channel_id=1, source_target_pairs={{0,3},{1,0},{2,1},{3,2},{4,7},{5,4},{6,5},{7,6},{8,11},{9,8},{10,9... | collective-permute-start | bytes 3145736 | tf_op jit(solution)/shard_map/ppermute | solution.py:249
  10.0 33.6 %all-to-all-start = ((f32[128,4,128]{2,1,0:T(4,128)}), f32[128,4,128]{2,1,0:T(4,128)S(1)}, u32[]{:S(2)}, u32[]{:S(2)}) async-start(f32[128,4,128]{2,1,0:T(4,128)} %broadcast_in_dim.8), calls=%async_computation | async-start | bytes 524288 | tf_op jit(solution)/shard_map/all_to_all | solution.py:24
  28.4 41.1 %collective-permute-start.2 = (bf16[1024,512]{1,0:T(8,128)(2,1)S(1)}, bf16[1024,512]{1,0:T(8,128)(2,1)}, u32[]{:S(2)}, u32[]{:S(2)}) collective-permute-start(bf16[1024,512]{1,0:T(8,128)(2,1)S(1)} %get-tuple-element.27.refs_0_), channel_id=1, source_target_pairs={{0,3},{1,0},{2,1},{3,2},{4,7},{5,4},{6,5},{7,6},{8,11},{9,8},{10,9... | collective-permute-start | bytes 3145736 | tf_op jit(solution)/shard_map/ppermute | solution.py:251
  31.6 42.3 %collective-permute-start.3 = (bf16[1024,512]{1,0:T(8,128)(2,1)S(1)}, bf16[1024,512]{1,0:T(8,128)(2,1)}, u32[]{:S(2)}, u32[]{:S(2)}) collective-permute-start(bf16[1024,512]{1,0:T(8,128)(2,1)S(1)} %get-tuple-element.28.refs_3_.refs_4_), channel_id=1, source_target_pairs={{0,1},{1,2},{2,3},{3,0},{4,5},{5,6},{6,7},{7,4},{8,9},{9,10},{10,1... | collective-permute-start | bytes 3145736 | tf_op jit(solution)/shard_map/ppermute | solution.py:250
  44.4 19.1 %all-to-all-start.1 = ((f32[4,4,128]{2,1,0:T(4,128)}), f32[4,4,128]{2,1,0:T(4,128)S(1)}, u32[]{:S(2)}, u32[]{:S(2)}) async-start(f32[4,4,128]{2,1,0:T(4,128)} %broadcast_in_dim.18), calls=%async_computation.1 | async-start | bytes 16384 | tf_op jit(solution)/shard_map/all_to_all | solution.py:24
  54.9 24.1 %collective-permute-start.4 = (bf16[768,512]{1,0:T(8,128)(2,1)}, bf16[768,512]{1,0:T(8,128)(2,1)}, u32[]{:S(2)}, u32[]{:S(2)}) collective-permute-start(bf16[768,512]{1,0:T(8,128)(2,1)} %slice.20), channel_id=1, source_target_pairs={{0,1},{1,2},{2,3},{3,0},{4,5},{5,6},{6,7},{7,4},{8,9},{9,10},{10,1... | collective-permute-start | bytes 2359304 | tf_op jit(solution)/shard_map/ppermute | solution.py:257
  58.2 20.8 %collective-permute-start.6 = (bf16[768,512]{1,0:T(8,128)(2,1)}, bf16[768,512]{1,0:T(8,128)(2,1)}, u32[]{:S(2)}, u32[]{:S(2)}) collective-permute-start(bf16[768,512]{1,0:T(8,128)(2,1)} %slice.22), channel_id=1, source_target_pairs={{0,3},{1,0},{2,1},{3,2},{4,7},{5,4},{6,5},{7,6},{8,11},{9,8},{10,9... | collective-permute-start | bytes 2359304 | tf_op jit(solution)/shard_map/ppermute | solution.py:258
  61.4 22.2 %collective-permute-start.5 = (bf16[256,512]{1,0:T(8,128)(2,1)}, bf16[256,512]{1,0:T(8,128)(2,1)S(1)}, u32[]{:S(2)}, u32[]{:S(2)}) collective-permute-start(bf16[256,512]{1,0:T(8,128)(2,1)} %slice.21), channel_id=1, source_target_pairs={{0,1},{1,2},{2,3},{3,0},{4,5},{5,6},{6,7},{7,4},{8,9},{9,10},{10,1... | collective-permute-start | bytes 786440 | tf_op jit(solution)/shard_map/ppermute | solution.py:259
  64.9 0.8 copy-start.1
  69.5 14.6 %collective-permute-start.7 = (bf16[256,512]{1,0:T(8,128)(2,1)}, bf16[256,512]{1,0:T(8,128)(2,1)S(1)}, u32[]{:S(2)}, u32[]{:S(2)}) collective-permute-start(bf16[256,512]{1,0:T(8,128)(2,1)} %slice.23), channel_id=1, source_target_pairs={{0,3},{1,0},{2,1},{3,2},{4,7},{5,4},{6,5},{7,6},{8,11},{9,8},{10,9... | collective-permute-start | bytes 786440 | tf_op jit(solution)/shard_map/ppermute | solution.py:260
  73.9 1.0 copy-start
  86.3 59.0 %copy-start.2 = (bf16[128,2048]{1,0:T(8,128)(2,1)S(1)}, bf16[128,2048]{1,0:T(8,128)(2,1)}, u32[]{:S(2)}) copy-start(bf16[128,2048]{1,0:T(8,128)(2,1)} %copy-done.1) | copy-start | bytes 1572868
